TPU v7x, 512 devices: a whole 4x4x16 slice. The times are simulated.
512 devices in a mesh: dp: 4 (over x), expert: 8 (over y, core), shard: 16 (over z).
Axes of the slice: x: 4, y: 4, z: 16, core: 2. Of those that a mesh axis runs over, the one named last changes fastest.
Arguments:
- output_gradient: bfloat16 [65536, 3072], P(('dp', 'expert', 'shard')), may hold values from -24 to 24
- saved_router_scores: float32 [65536, 8], P(('dp', 'expert', 'shard')), may hold values from -8 to 8
- expert_choice_index: int32 [65536, 2], P(('dp', 'expert', 'shard')), may hold values from 0 to 7, as said below
- router_matrix: bfloat16 [8, 3072], replicated, may hold values from -0.109375 to 0.109375
- weight_normalized_entries: bfloat16 [3072, 8192], P('shard', 'expert'), may hold values from -1 to 1
- scales: bfloat16 [48, 8192], P('shard', 'expert'), may hold values from 0.0099487305 to 0.099609375
- stored_hidden_state: bfloat16 [4, 16, 256, 8192], P('dp', 'shard', None, 'expert'), may hold values from -6 to 6
- context: bfloat16 [65536, 3072], P(('dp', 'expert', 'shard')), may hold values from -6 to 6
- adapter_down_factor: bfloat16 [64, 3072], replicated, may hold values from -0.109375 to 0.109375
- adapter_up_factor: bfloat16 [64, 3072], replicated, may hold values from -0.109375 to 0.109375
Outputs:
- hidden_grad: bfloat16 [4, 16, 256, 8192], P('dp', 'shard', None, 'expert')
- token_grad: bfloat16 [65536, 3072], P(('dp', 'expert', 'shard'))
- grad_down: float32 [64, 3072], P(None, 'shard')
- up_factor_gradient: float32 [64, 3072], P(None, 'shard')
Inputs may be any that keep to these rules, and one draw needn't show every extreme that they name: `expert_choice_index`: each token names two different experts and expert 0 at most once. The 128 tokens of one device block name expert 0 at most 32 times, and in every draw all device blocks of some pair of dp and shard indices name it exactly 32 times.
All inputs are finite; a program needn't handle non-finite values.
Results may differ from a plain program's by a relative error of at most 0.015.
Values may be sent and summed in bfloat16 or wider, within the bound.
A program may use at most 64 MiB of HBM per device.

v0:
```python
import jax
import jax.numpy as jnp
from jax import lax
from jax.sharding import PartitionSpec as P

ADAPTER_SCALE = 0.25


def per_device(
    output_gradient,
    saved_router_scores,
    expert_choice_index,
    router_matrix,
    weight_normalized_entries,
    scales,
    stored_hidden_state,
    context,
    adapter_down_factor,
    adapter_up_factor,
):
    expert_count = lax.axis_size("expert")
    shard_count = lax.axis_size("shard")
    tokens, feature_width = output_gradient.shape
    experts = saved_router_scores.shape[1]
    row_count = stored_hidden_state.shape[2]
    capacity = row_count // expert_count
    ff_share = stored_hidden_state.shape[3]
    block_size = weight_normalized_entries.shape[0] // scales.shape[0]
    labels = jnp.arange(experts, dtype=jnp.int32)
    choose = expert_choice_index[:, :, None] == labels[None, None, :]
    chosen = jnp.sum(jnp.where(choose, saved_router_scores[:, None, :], 0.0), axis=2)
    first_prob = 1.0 / (1.0 + jnp.exp(chosen[:, 1] - chosen[:, 0]))
    second_prob = 1.0 - first_prob
    in_window = expert_choice_index == 0
    window_flag = jnp.any(in_window, axis=1)
    flag_int = window_flag.astype(jnp.int32)
    slot_index = jnp.cumsum(flag_int) - flag_int
    route_probs = jnp.stack([first_prob, second_prob], axis=1).astype(jnp.bfloat16)
    window_prob = jnp.where(in_window[:, 0], route_probs[:, 0], route_probs[:, 1])
    slot_labels = jnp.arange(capacity, dtype=jnp.int32)
    placement = (window_flag[None, :] & (slot_index[None, :] == slot_labels[:, None])).astype(
        jnp.bfloat16
    )
    send_rows = jnp.dot(placement, output_gradient, preferred_element_type=jnp.float32).astype(
        jnp.bfloat16
    )
    send_probs = jnp.dot(placement, window_prob, preferred_element_type=jnp.float32).astype(
        jnp.bfloat16
    )
    all_rows, all_probs = (
        lax.all_gather(send_rows, "expert", axis=0, tiled=True),
        lax.all_gather(send_probs, "expert", axis=0, tiled=True),
    )
    code_blocks = weight_normalized_entries.reshape(scales.shape[0], block_size, ff_share)
    own_weight = (
        (code_blocks.astype(jnp.float32) * scales.astype(jnp.float32)[:, None, :])
        .astype(jnp.bfloat16)
        .reshape(weight_normalized_entries.shape[0], ff_share)
    )
    product = jnp.dot(
        all_rows,
        lax.all_gather(own_weight, "shard", axis=0, tiled=True),
        preferred_element_type=jnp.float32,
    )
    hidden_grad = (all_probs.astype(jnp.float32)[:, None] * product).astype(jnp.bfloat16)
    partial_value = jnp.sum(stored_hidden_state[0, 0].astype(jnp.float32) * product, axis=1)
    returned = lax.psum_scatter(partial_value, "expert", scatter_dimension=0, tiled=True)
    window_grad = jnp.where(window_flag, returned[jnp.minimum(slot_index, capacity - 1)], 0.0)
    pair_grad = jnp.where(in_window, window_grad[:, None], 0.0)
    spread = first_prob * second_prob * (pair_grad[:, 0] - pair_grad[:, 1])
    sign_table = choose[:, 0, :].astype(jnp.float32) - choose[:, 1, :].astype(jnp.float32)
    logit_grad = (spread[:, None] * sign_table).astype(jnp.bfloat16)
    token_grad = jnp.dot(logit_grad, router_matrix, preferred_element_type=jnp.float32).astype(
        jnp.bfloat16
    )
    token_kept = lax.optimization_barrier(token_grad)
    residual_gradient = (
        output_gradient.astype(jnp.float32) + token_kept.astype(jnp.float32)
    ).astype(jnp.bfloat16)
    narrow_input = lax.dot_general(
        context, adapter_down_factor, (((1,), (1,)), ((), ())), preferred_element_type=jnp.float32
    ).astype(jnp.bfloat16)
    narrow_gradient = (
        ADAPTER_SCALE
        * lax.dot_general(
            residual_gradient,
            adapter_up_factor,
            (((1,), (1,)), ((), ())),
            preferred_element_type=jnp.float32,
        )
    ).astype(jnp.bfloat16)
    partial_up_gradient = ADAPTER_SCALE * lax.dot_general(
        narrow_input,
        residual_gradient,
        (((0,), (0,)), ((), ())),
        preferred_element_type=jnp.float32,
    )
    part_down = lax.dot_general(
        narrow_gradient, context, (((0,), (0,)), ((), ())), preferred_element_type=jnp.float32
    )
    summed_up, summed_down = lax.psum((partial_up_gradient, part_down), ("dp", "expert", "shard"))
    share_width = feature_width // shard_count
    first_col = lax.axis_index("shard") * share_width
    up_factor_gradient = lax.dynamic_slice_in_dim(summed_up, first_col, share_width, 1)
    grad_down = lax.dynamic_slice_in_dim(summed_down, first_col, share_width, 1)
    return (
        hidden_grad.reshape(stored_hidden_state.shape),
        token_grad,
        grad_down,
        up_factor_gradient,
    )


def solution(mesh):
    in_specs = (
        P(("dp", "expert", "shard"), None),
        P(("dp", "expert", "shard"), None),
        P(("dp", "expert", "shard"), None),
        P(),
        P("shard", "expert"),
        P("shard", "expert"),
        P("dp", "shard", None, "expert"),
        P(("dp", "expert", "shard"), None),
        P(),
        P(),
    )
    out_specs = (
        P("dp", "shard", None, "expert"),
        P(("dp", "expert", "shard"), None),
        P(None, "shard"),
        P(None, "shard"),
    )
    return jax.shard_map(
        per_device, mesh=mesh, in_specs=in_specs, out_specs=out_specs, check_vma=False
    )
```

profile of v0, /device:TPU:1, one launch (start us, length us, event | category | flops | bytes accessed | tf_op | source)
XLA Modules:
  0.0 639.2 jit_solution(14666868364817851319)
XLA Ops:
  7.2 0.0 copy-start
  7.2 0.0 copy-start.7
  7.2 0.0 copy-start.5
  7.2 0.0 copy-start.3
  7.2 0.0 copy-start.6
  7.2 0.0 copy-start.8
  7.2 0.0 all-gather.3.cloned.1.call-start
  7.3 0.8 fusion.24
  8.1 0.1 copy.26
  8.2 0.2 reduce-window.4
  8.4 0.1 fusion.6
  8.5 2.0 convolution_convert_fusion.1
  10.6 0.0 all-gather.3.cloned.1.call-update
  10.6 0.0 all-gather.5.cloned.1.call-start
  10.6 0.7 convert_element_type.90
  11.3 0.0 copy-done.3
  11.3 0.8 fusion.4
  12.2 0.0 all-gather.5.cloned.1.call-update
  12.2 0.0 all-reduce.5.cloned.1.call-start
  12.3 0.0 copy-done.7
  12.3 0.6 fusion.25
  13.5 0.0 copy-done.5
  13.5 0.0 copy-done.6
  13.6 0.0 copy-start.4
  13.6 35.0 %all-gather.3.cloned.1.call-done = bf16[256,3072]{1,0:T(8,128)(2,1)} async-done(((bf16[32,3072]{1,0:T(8,128)(2,1)}), bf16[256,3072]{1,0:T(8,128)(2,1)}) %all-gather.3.cloned.1.call-update) | async-done | bytes 1572880 | tf_op jit(solution)/shard_map/all_gather | solution.py:51
  48.5 86.7 %all-gather.5.cloned.1.call-done = bf16[3072,1024]{1,0:T(8,128)(2,1)} async-done(((bf16[192,1024]{1,0:T(8,128)(2,1)}), bf16[3072,1024]{1,0:T(8,128)(2,1)}) %all-gather.5.cloned.1.call-update) | async-done | bytes 6291472 | tf_op jit(solution)/shard_map/all_gather | solution.py:62
  135.2 0.0 copy-done.8
  135.2 5.2 fusion.3
  140.4 0.0 copy-start.1
  140.4 14.6 %all-reduce.1 = f32[256]{0:T(256)S(1)} all-reduce(f32[256]{0:T(256)S(1)} %get-tuple-element.14), channel_id=2, replica_groups=mesh['dp'=4,'expert'=8,'shard'=16] {'expert'}, use_global_device_ids=true, to_apply=%region_4.5.clone | all-reduce | flops 256 | bytes 2048
  155.0 0.1 dynamic-slice.2
  155.1 1.2 gather_fusion
  156.3 0.0 copy-done.4
  156.3 0.4 convolution_convert_fusion
  156.8 0.0 copy-done
  156.8 0.0 copy-done.1
  156.8 0.0 copy-start.2
  156.8 3.0 convolution_multiply_fusion
  159.8 0.0 copy-done.2
  159.8 2.7 fusion.1
  162.4 0.0 all-reduce.5.cloned.1.call-update
  163.1 0.1 fusion.2
  163.2 0.2 dynamic-update-slice
  163.4 12.6 %all-reduce = bf16[256]{0:T(256)(128)(2,1)S(1)} all-reduce(bf16[256]{0:T(256)(128)(2,1)S(1)} %dynamic-update-slice), channel_id=1, replica_groups=mesh['dp'=4,'expert'=8,'shard'=16] {'expert'}, use_global_device_ids=true, to_apply=%add | all-reduce | flops 256 | bytes 1024
  176.1 0.9 fusion.5
  177.0 454.0 %all-reduce.5.cloned.1.call-done = (f32[64,3072]{1,0:T(8,128)}, f32[64,3072]{1,0:T(8,128)}) async-done(((f32[64,3072]{1,0:T(8,128)}, f32[64,3072]{1,0:T(8,128)}), (f32[64,3072]{1,0:T(8,128)}, f32[64,3072]{1,0:T(8,128)})) %all-reduce.5.cloned.1.call-update) | async-done | bytes 1572880 | tf_op jit(solution)/shard_map/psum | solution.py:101
  630.9 1.7 constant_dynamic-slice_fusion
  (10 shorter events, 0.1 us)
Async XLA Ops:
  7.2 149.6 %copy-start = (bf16[128,3072]{1,0:T(8,128)(2,1)S(1)}, bf16[128,3072]{1,0:T(8,128)(2,1)}, u32[]{:S(2)}) copy-start(bf16[128,3072]{1,0:T(8,128)(2,1)} %param.17) | copy-start | bytes 2359300
  7.2 5.1 copy-start.7
  7.2 6.3 copy-start.5
  7.2 4.1 copy-start.3
  7.2 6.3 copy-start.6
  7.2 128.0 %copy-start.8 = (bf16[1,1,256,1024]{3,2,1,0:T(8,128)(2,1)S(1)}, bf16[1,1,256,1024]{3,2,1,0:T(8,128)(2,1)}, u32[]{:S(2)}) copy-start(bf16[1,1,256,1024]{3,2,1,0:T(8,128)(2,1)} %param.16) | copy-start | bytes 1572868
  7.2 41.3 %all-gather.3.cloned.1.call-start = ((), (), s32[]{:S(2)}) async-start(), calls=%async_computation | async-start | bytes 1769472 | tf_op jit(solution)/shard_map/all_gather | solution.py:51
  10.6 124.6 %all-gather.5.cloned.1.call-start = ((), (), s32[]{:S(2)}) async-start(), calls=%async_computation.1 | async-start | bytes 6684672 | tf_op jit(solution)/shard_map/all_gather | solution.py:62
  12.2 618.7 %all-reduce.5.cloned.1.call-start = ((), (), s32[]{:S(2)}) async-start(), calls=%async_computation.2 | async-start | bytes 3145728 | tf_op jit(solution)/shard_map/psum | solution.py:101
  13.6 142.8 %copy-start.4 = (bf16[8,3072]{1,0:T(8,128)(2,1)S(1)}, bf16[8,3072]{1,0:T(8,128)(2,1)}, u32[]{:S(2)}) copy-start(bf16[8,3072]{1,0:T(8,128)(2,1)} %param.13) | copy-start | bytes 147460
  140.4 16.4 %copy-start.1 = (bf16[128,3072]{1,0:T(8,128)(2,1)S(1)}, bf16[128,3072]{1,0:T(8,128)(2,1)}, u32[]{:S(2)}) copy-start(bf16[128,3072]{1,0:T(8,128)(2,1)} %param.10) | copy-start | bytes 2359300
  156.8 3.0 copy-start.2
Sparse Core Ops, SparseCore 0:
  10.8 37.7 all-gather.2
  51.2 83.9 all-gather.4
  162.6 468.3 all-reduce.4
where the time goes:
time: 640 us; the launch traced here: 639 us
  waiting for transfers between devices  576 us (90%)
  blocking collectives  27.2 us (4%)
  between operations  15.2 us (2%)
  matrix products  13.4 us (2%)
    psum x1, waiting for transfers between devices, per_device(): lax.psum((partial_up_gradient, part_down), ('dp', 'expert', 'shard'))  454 us
    all_gather x1, waiting for transfers between devices, per_device(): lax.all_gather(own_weight, 'shard', axis=0, tiled=True)  86.7 us
    all_gather x1, waiting for transfers between devices, per_device(): lax.all_gather(send_rows, 'expert', axis=0, tiled=True)  35 us
    unnamed x2, blocking collectives  27.2 us
  transfers between devices with their start and end apart: 3, of which 3 were waited for; matrix products, arithmetic and copies ran while one was open for 1% of the time, Pallas kernels for 0%

commit v1 on v0

--- a/solution.py
+++ b/solution.py
@@ -1,9 +1,163 @@
 import jax
 import jax.numpy as jnp
 from jax import lax
+from jax.experimental import pallas as pl
+from jax.experimental.pallas import tpu as pltpu
 from jax.sharding import PartitionSpec as P
 
+MESH = pl.DeviceIdType.MESH
+
 ADAPTER_SCALE = 0.25
+
+
+def reduce_kernel(
+    a_ref, out_ref, twin_in, y_out, y_in, x_out, x_in, z_out, z_in, fin, send, recv
+):
+    d, e, s = lax.axis_index("dp"), lax.axis_index("expert"), lax.axis_index("shard")
+    y, c = e // 2, e % 2
+    flat = d * 8 + e
+
+    barrier = pltpu.get_barrier_semaphore()
+    for p in range(1, 32):
+        q = (flat + p) % 32
+        pl.semaphore_signal(barrier, inc=1, device_id=(q // 8, q % 8, s), device_id_type=MESH)
+    for p in range(1, 16):
+        pl.semaphore_signal(barrier, inc=1, device_id=(d, e, (s + p) % 16), device_id_type=MESH)
+    pl.semaphore_wait(barrier, 46)
+
+    def copy(src, dst, i, j, target):
+        return pltpu.make_async_remote_copy(
+            src_ref=src,
+            dst_ref=dst,
+            send_sem=send.at[i],
+            recv_sem=recv.at[j],
+            device_id=target,
+            device_id_type=MESH,
+        )
+
+    half = a_ref.shape[1] // 2
+    twin = (d, y * 2 + 1 - c, s)
+    other = pl.ds(pl.multiple_of((1 - c) * half, half), half)
+    mine = pl.ds(pl.multiple_of(c * half, half), half)
+    first = copy(a_ref.at[:, other], twin_in, 0, 0, twin)
+    first.start()
+    first.wait()
+    twin_in[...] += a_ref[:, mine]
+
+    y_out[...] = twin_in[...].astype(jnp.bfloat16)
+    sends = []
+    for j in range(1, 4):
+        to = (y + j) % 4
+        sends.append(
+            copy(
+                y_out.at[pl.ds(pl.multiple_of(to * 32, 32), 32)],
+                y_in.at[j - 1],
+                j,
+                j,
+                (d, to * 2 + c, s),
+            )
+        )
+    for one in sends:
+        one.start()
+    for one in sends:
+        one.wait()
+    x_out[...] = twin_in[pl.ds(pl.multiple_of(y * 32, 32), 32), :]
+    for j in range(3):
+        x_out[...] += y_in[j].astype(jnp.float32)
+
+    sends = []
+    for j in range(1, 4):
+        to = (d + j) % 4
+        sends.append(
+            copy(
+                x_out.at[pl.ds(pl.multiple_of(to * 8, 8), 8)],
+                x_in.at[j - 1],
+                3 + j,
+                3 + j,
+                (to, e, s),
+            )
+        )
+    for one in sends:
+        one.start()
+    for one in sends:
+        one.wait()
+    part = x_out[pl.ds(pl.multiple_of(d * 8, 8), 8), :] + x_in[0] + x_in[1] + x_in[2]
+
+    for j in range(8):
+        z_out[j, :, 0:192] = part[:, 192 * j : 192 * j + 192]
+    z_out[:, :, 192:256] = jnp.zeros((8, 8, 64), jnp.float32)
+    keeps = s // 8 == c
+    for j in range(8):
+        k = c * 8 + j
+
+        @pl.when(k != s)
+        def _():
+            copy(z_out.at[j], z_in.at[s], 7 + j, 7 + s, (d, e, k)).start()
+
+    @pl.when(keeps)
+    def _():
+        z_in[s] = z_out[s % 8]
+        for i in range(16):
+
+            @pl.when(i != s)
+            def _():
+                copy(z_out.at[0], z_in.at[i], 7, 7 + i, (d, e, (s + 1) % 16)).wait_recv()
+
+        total = z_in[0]
+        for i in range(1, 16):
+            total = total + z_in[i]
+        fin[y * 4 + d] = total
+        for p in range(1, 32):
+            q = (flat + p) % 32
+            slot = y * 4 + d
+            copy(
+                fin.at[slot], fin.at[slot], 14 + p, 23 + slot, (q // 8, q % 8, s)
+            ).start()
+
+    for t in range(16):
+
+        @pl.when((t != y * 4 + d) | jnp.logical_not(keeps))
+        def _():
+            copy(fin.at[t], fin.at[t], 0, 23 + t, twin).wait_recv()
+
+    for j in range(8):
+
+        @pl.when(c * 8 + j != s)
+        def _():
+            copy(z_out.at[j], z_in.at[j], 7 + j, 7, twin).wait_send()
+
+    @pl.when(keeps)
+    def _():
+        for p in range(1, 32):
+            copy(fin.at[0], fin.at[0], 14 + p, 23, twin).wait_send()
+
+    for t in range(16):
+        out_ref[8 * t : 8 * t + 8, :] = fin[t, :, 0:192]
+
+
+def reduce_all(stacked):
+    f32 = jnp.float32
+    return pl.pallas_call(
+        reduce_kernel,
+        out_shape=jax.ShapeDtypeStruct((128, 192), f32),
+        in_specs=[pl.BlockSpec(memory_space=pltpu.VMEM)],
+        out_specs=pl.BlockSpec(memory_space=pltpu.VMEM),
+        scratch_shapes=[
+            pltpu.VMEM((128, 1536), f32),
+            pltpu.VMEM((128, 1536), jnp.bfloat16),
+            pltpu.VMEM((3, 32, 1536), jnp.bfloat16),
+            pltpu.VMEM((32, 1536), f32),
+            pltpu.VMEM((3, 8, 1536), f32),
+            pltpu.VMEM((8, 8, 256), f32),
+            pltpu.VMEM((16, 8, 256), f32),
+            pltpu.VMEM((16, 8, 256), f32),
+            pltpu.SemaphoreType.DMA((46,)),
+            pltpu.SemaphoreType.DMA((39,)),
+        ],
+        compiler_params=pltpu.CompilerParams(
+            collective_id=0, has_side_effects=True, vmem_limit_bytes=32 << 20
+        ),
+    )(stacked)
 
 
 def per_device(
@@ -19,8 +173,7 @@
     adapter_up_factor,
 ):
     expert_count = lax.axis_size("expert")
-    shard_count = lax.axis_size("shard")
-    tokens, feature_width = output_gradient.shape
+    tokens = output_gradient.shape[0]
     experts = saved_router_scores.shape[1]
     row_count = stored_hidden_state.shape[2]
     capacity = row_count // expert_count
@@ -34,7 +187,10 @@
     in_window = expert_choice_index == 0
     window_flag = jnp.any(in_window, axis=1)
     flag_int = window_flag.astype(jnp.int32)
-    slot_index = jnp.cumsum(flag_int) - flag_int
+    positions = jnp.arange(tokens, dtype=jnp.int32)
+    slot_index = jnp.sum(
+        jnp.where(positions[None, :] < positions[:, None], flag_int[None, :], 0), axis=1
+    )
     route_probs = jnp.stack([first_prob, second_prob], axis=1).astype(jnp.bfloat16)
     window_prob = jnp.where(in_window[:, 0], route_probs[:, 0], route_probs[:, 1])
     slot_labels = jnp.arange(capacity, dtype=jnp.int32)
@@ -98,11 +254,9 @@
     part_down = lax.dot_general(
         narrow_gradient, context, (((0,), (0,)), ((), ())), preferred_element_type=jnp.float32
     )
-    summed_up, summed_down = lax.psum((partial_up_gradient, part_down), ("dp", "expert", "shard"))
-    share_width = feature_width // shard_count
-    first_col = lax.axis_index("shard") * share_width
-    up_factor_gradient = lax.dynamic_slice_in_dim(summed_up, first_col, share_width, 1)
-    grad_down = lax.dynamic_slice_in_dim(summed_down, first_col, share_width, 1)
+    summed = reduce_all(jnp.concatenate([partial_up_gradient, part_down], axis=0))
+    up_factor_gradient = summed[:64]
+    grad_down = summed[64:]
     return (
         hidden_grad.reshape(stored_hidden_state.shape),
         token_grad,

time: 640 us -> 221 us (0.35)
  waiting for transfers between devices: 576 us -> 120 us
  Pallas kernels: 0 us -> 36.3 us
    psum x1 -> x0, waiting for transfers between devices: 454 us -> none  [per_device(): lax.psum((partial_up_gradient, part_down), ('dp', 'expert', 'shard'))]
    pallas_call x0 -> x1, Pallas kernels: none -> 36.3 us  [reduce_all(): pl.pallas_call(reduce_kernel, out_shape=jax.ShapeDtypeStruct((128, 192),...]
  transfers between devices with their start and end apart: 3 -> 2, of which waited for: 3 -> 2; matrix products, arithmetic and copies ran while one was open for 1% -> 1% of each run, Pallas kernels for 0% -> 0%
where the time goes in v1:
time: 221 us; the launch traced here: 220 us
  waiting for transfers between devices  120 us (54%)
  Pallas kernels  36.3 us (16%)
  blocking collectives  26.8 us (12%)
  between operations  15.6 us (7%)
  matrix products  12.1 us (5%)
  other arithmetic  5.7 us (3%)
  local copies, waits for them, and re-layouts  2.89 us (1%)
    all_gather x1, waiting for transfers between devices, per_device(): lax.all_gather(own_weight, 'shard', axis=0, tiled=True)  86.7 us
    pallas_call x1, Pallas kernels, reduce_all(): pl.pallas_call(reduce_kernel, out_shape=jax.ShapeDtypeStruct((128, 192),...  36.3 us
    all_gather x1, waiting for transfers between devices, per_device(): lax.all_gather(send_rows, 'expert', axis=0, tiled=True)  33.7 us
    unnamed x2, blocking collectives  26.8 us
    dot_general x1, matrix products, per_device(): jnp.dot(all_rows, lax.all_gather(own_weight, 'shard', axis=0, tiled=True)...  6.14 us
  transfers between devices with their start and end apart: 2, of which 2 were waited for; matrix products, arithmetic and copies ran while one was open for 1% of the time, Pallas kernels for 0%

profile of v1, /device:TPU:1, one launch (start us, length us, event | category | flops | bytes accessed | tf_op | source)
XLA Modules:
  0.0 219.8 jit_solution(9933695371071443783)
XLA Ops:
  7.2 0.0 copy-start
  7.2 0.0 copy-start.8
  7.2 0.0 copy-start.6
  7.2 0.0 copy-start.7
  7.2 0.0 copy-start.9
  7.2 0.0 all-gather.3.cloned.1.call-start
  7.3 0.8 fusion.24
  8.1 0.1 select_reduce_fusion
  8.2 2.1 convolution_convert_fusion.1
  10.2 0.0 all-gather.3.cloned.1.call-update
  10.3 0.0 all-gather.5.cloned.1.call-start
  10.3 0.7 convert_element_type.72
  11.0 1.8 fusion.4
  12.8 0.0 all-gather.5.cloned.1.call-update
  12.9 0.0 copy-done.8
  12.9 0.6 fusion.26
  14.8 0.0 copy-done.6
  14.8 0.0 copy-done.7
  14.8 0.0 copy-start.5
  14.9 33.7 %all-gather.3.cloned.1.call-done = bf16[256,3072]{1,0:T(8,128)(2,1)} async-done(((bf16[32,3072]{1,0:T(8,128)(2,1)}), bf16[256,3072]{1,0:T(8,128)(2,1)}) %all-gather.3.cloned.1.call-update) | async-done | bytes 1572880 | tf_op jit(solution)/shard_map/all_gather | solution.py:207
  48.5 86.7 %all-gather.5.cloned.1.call-done = bf16[3072,1024]{1,0:T(8,128)(2,1)} async-done(((bf16[192,1024]{1,0:T(8,128)(2,1)}), bf16[3072,1024]{1,0:T(8,128)(2,1)}) %all-gather.5.cloned.1.call-update) | async-done | bytes 6291472 | tf_op jit(solution)/shard_map/all_gather | solution.py:218
  135.2 0.0 copy-done.9
  135.2 6.1 %fusion.3 = (f32[256]{0:T(256)S(1)}, f32[256,1024]{1,0:T(8,128)}) fusion(bf16[1,1,256,1024]{3,2,1,0:T(8,128)(2,1)S(1)} %copy-done.9, bf16[256,3072]{1,0:T(8,128)(2,1)} %all-gather.3.cloned.1.call-done, bf16[3072,1024]{1,0:T(8,128)(2,1)} %all-gather.5.cloned.1.call-done), kind=kOutput, calls=%fused_computation.13 | convolution fusion | flops 1611398912 | bytes 9438208 | tf_op jit(solution)/shard_map/dot_general | solution.py:216
  141.3 0.0 copy-start.1
  141.3 0.0 copy-start.4
  141.3 14.6 %all-reduce.1 = f32[256]{0:T(256)S(1)} all-reduce(f32[256]{0:T(256)S(1)} %get-tuple-element.12), channel_id=2, replica_groups=mesh['dp'=4,'expert'=8,'shard'=16] {'expert'}, use_global_device_ids=true, to_apply=%region_4.5.clone | all-reduce | flops 256 | bytes 2048
  155.9 0.1 dynamic-slice.2
  156.0 1.2 gather_fusion
  157.3 0.0 copy-done.5
  157.3 0.4 convolution_convert_fusion
  157.7 0.0 copy-done
  157.7 0.0 copy-done.1
  157.7 0.0 copy-done.4
  157.7 0.0 copy-start.2
  157.8 0.8 convolution_multiply_fusion
  158.5 0.1 copy-done.2
  158.6 2.7 %fusion.1 = f32[64,3072]{1,0:T(8,128)} fusion(bf16[128,3072]{1,0:T(8,128)(2,1)S(1)} %copy-done, bf16[64,3072]{1,0:T(8,128)(2,1)} %param.19, bf16[128,3072]{1,0:T(8,128)(2,1)S(1)} %convolution_convert_fusion, bf16[128,3072]{1,0:T(8,128)(2,1)S(1)} %copy-done.1), kind=kOutput, calls=%fused_computation.9 | convolution fusion | flops 102252544 | bytes 3538944 | tf_op jit(solution)/shard_map/dot_general | solution.py:254
  161.3 1.3 pad_maximum_fusion.a_ref
  162.6 0.0 copy-start.3
  162.6 36.3 %shard_map.129 = f32[128,192]{1,0:T(8,128)S(1)} custom-call(f32[128,3072]{1,0:T(8,128)S(1)} %pad_maximum_fusion.a_ref), custom_call_target="tpu_custom_call" | custom-call | tf_op jit(solution)/shard_map/pallas_call | solution.py:140
  198.9 0.7 fusion.25
  199.5 0.1 fusion.2
  199.6 0.2 dynamic-update-slice
  199.8 12.2 %all-reduce = bf16[256]{0:T(256)(128)(2,1)S(1)} all-reduce(bf16[256]{0:T(256)(128)(2,1)S(1)} %dynamic-update-slice), channel_id=1, replica_groups=mesh['dp'=4,'expert'=8,'shard'=16] {'expert'}, use_global_device_ids=true, to_apply=%add | all-reduce | flops 256 | bytes 1024
  212.0 0.0 copy-done.3
  212.0 0.9 fusion.5
  (10 shorter events, 0.1 us)
Async XLA Ops:
  7.2 150.6 %copy-start = (bf16[128,3072]{1,0:T(8,128)(2,1)S(1)}, bf16[128,3072]{1,0:T(8,128)(2,1)}, u32[]{:S(2)}) copy-start(bf16[128,3072]{1,0:T(8,128)(2,1)} %param.17) | copy-start | bytes 2359300
  7.2 5.7 %copy-start.8 = (u32[512]{0:T(512)S(1)}, u32[512]{0:T(512)}, u32[]{:S(2)}) copy-start(u32[512]{0:T(512)} %constant.25) | copy-start | bytes 6148
  7.2 7.6 %copy-start.6 = (s32[128,2]{0,1:T(2,128)S(1)}, s32[128,2]{0,1:T(2,128)}, u32[]{:S(2)}) copy-start(s32[128,2]{0,1:T(2,128)} %param.12) | copy-start | bytes 3076
  7.2 7.6 %copy-start.7 = (f32[128,8]{0,1:T(8,128)S(1)}, f32[128,8]{0,1:T(8,128)}, u32[]{:S(2)}) copy-start(f32[128,8]{0,1:T(8,128)} %param.11) | copy-start | bytes 12292
  7.2 128.0 %copy-start.9 = (bf16[1,1,256,1024]{3,2,1,0:T(8,128)(2,1)S(1)}, bf16[1,1,256,1024]{3,2,1,0:T(8,128)(2,1)}, u32[]{:S(2)}) copy-start(bf16[1,1,256,1024]{3,2,1,0:T(8,128)(2,1)} %param.16) | copy-start | bytes 1572868
  7.2 41.3 %all-gather.3.cloned.1.call-start = ((), (), s32[]{:S(2)}) async-start(), calls=%async_computation | async-start | bytes 1769472 | tf_op jit(solution)/shard_map/all_gather | solution.py:207
  10.3 124.9 %all-gather.5.cloned.1.call-start = ((), (), s32[]{:S(2)}) async-start(), calls=%async_computation.1 | async-start | bytes 6684672 | tf_op jit(solution)/shard_map/all_gather | solution.py:218
  14.8 142.4 %copy-start.5 = (bf16[8,3072]{1,0:T(8,128)(2,1)S(1)}, bf16[8,3072]{1,0:T(8,128)(2,1)}, u32[]{:S(2)}) copy-start(bf16[8,3072]{1,0:T(8,128)(2,1)} %param.13) | copy-start | bytes 147460
  141.3 16.4 %copy-start.1 = (bf16[128,3072]{1,0:T(8,128)(2,1)S(1)}, bf16[128,3072]{1,0:T(8,128)(2,1)}, u32[]{:S(2)}) copy-start(bf16[128,3072]{1,0:T(8,128)(2,1)} %param.10) | copy-start | bytes 2359300
  141.3 16.4 %copy-start.4 = (bf16[64,3072]{1,0:T(8,128)(2,1)S(1)}, bf16[64,3072]{1,0:T(8,128)(2,1)}, u32[]{:S(2)}) copy-start(bf16[64,3072]{1,0:T(8,128)(2,1)} %param.18) | copy-start | bytes 1179652
  157.7 0.9 copy-start.2
  162.6 49.5 %copy-start.3 = (f32[256,1024]{1,0:T(8,128)S(1)}, f32[256,1024]{1,0:T(8,128)}, u32[]{:S(2)}) copy-start(f32[256,1024]{1,0:T(8,128)} %get-tuple-element.13) | copy-start | bytes 3145732
Sparse Core Ops, SparseCore 0:
  10.8 37.7 all-gather.2
  51.2 83.9 all-gather.4

commit v2 on v0

v2 whole, which is shorter than its diff:
```python
import jax
import jax.numpy as jnp
from jax import lax
from jax.experimental import pallas as pl
from jax.experimental.pallas import tpu as pltpu
from jax.sharding import PartitionSpec as P

ADAPTER_SCALE = 0.25
MESH = pl.DeviceIdType.MESH
F32, BF16 = jnp.float32, jnp.bfloat16
FEATURES, TAIL, SLOTS, RANK = 3072, 128, 32, 64
SENDS, RECVS = 110, 130


def dot(a, b, over, precision=None):
    return lax.dot_general(
        a, b, ((over[:1], over[1:]), ((), ())), precision=precision, preferred_element_type=F32
    )


def layer_kernel(
    og,
    scores,
    idx,
    router,
    codes,
    scales,
    stored,
    ctx,
    down,
    up,
    hidden_out,
    token_out,
    up_out,
    down_out,
    rows,
    weight,
    prod_out,
    prod_in,
    hidden,
    token,
    pg_out,
    pg_in,
    adapt,
    a_twin,
    a_y_out,
    a_y_in,
    a_x_out,
    a_x_in,
    a_z_out,
    a_z_in,
    b_pad,
    b_twin,
    b_z_out,
    b_z_in,
    y_gather,
    x_gather,
    router_pad,
    send,
    recv,
    local,
):
    d, e, s = lax.axis_index("dp"), lax.axis_index("expert"), lax.axis_index("shard")
    y, c = e // 2, e % 2
    twin = (d, y * 2 + 1 - c, s)
    keeps = s // 8 == c

    barrier = pltpu.get_barrier_semaphore()
    for target in (
        twin,
        ((d + 1) % 4, e, s),
        ((d + 3) % 4, e, s),
        (d, (e + 2) % 8, s),
        (d, (e + 6) % 8, s),
        (d, e, (s + 1) % 16),
        (d, e, (s + 15) % 16),
    ):
        pl.semaphore_signal(barrier, inc=1, device_id=target, device_id_type=MESH)

    made = []
    used = [0, 0]

    def describe(src, dst, i, j, target):
        return pltpu.make_async_remote_copy(
            src_ref=src,
            dst_ref=dst,
            send_sem=send.at[i],
            recv_sem=recv.at[j],
            device_id=target,
            device_id_type=MESH,
        )

    def start(src, dst, target):
        one = describe(src, dst, used[0], used[1], target)
        used[0] += 1
        used[1] += 1
        one.start()
        made.append(one)
        return one

    def row_range(first, count, step):
        return pl.ds(pl.multiple_of(first, step), count)

    quarter = pl.ds(pl.multiple_of(d * 256, 256), 256)
    factors = scales[:, quarter].astype(F32)
    for k in range(3):
        block = codes[64 * k : 64 * k + 64, quarter].astype(F32) * factors[k : k + 1, :]
        weight[row_range(s * 192 + 64 * k, 64, 64), :] = block.astype(BF16)

    labels = lax.broadcasted_iota(jnp.int32, (128, 8), 1)
    first_choice, second_choice = idx[:, 0:1], idx[:, 1:2]
    choose_first, choose_second = labels == first_choice, labels == second_choice
    score = scores[...]
    chosen_first = jnp.sum(jnp.where(choose_first, score, 0.0), axis=1, keepdims=True)
    chosen_second = jnp.sum(jnp.where(choose_second, score, 0.0), axis=1, keepdims=True)
    first_prob = 1.0 / (1.0 + jnp.exp(chosen_second - chosen_first))
    second_prob = 1.0 - first_prob
    in_first = (first_choice == 0).astype(F32)
    in_second = (second_choice == 0).astype(F32)
    flag = in_first + in_second
    before = lax.broadcasted_iota(jnp.int32, (128, 128), 0) > lax.broadcasted_iota(
        jnp.int32, (128, 128), 1
    )
    slot = dot(
        before.astype(BF16), jnp.broadcast_to(flag, (128, 128)).astype(BF16), (1, 0)
    )
    slot_labels = lax.broadcasted_iota(jnp.int32, (128, SLOTS), 1).astype(F32)
    placement = jnp.where(slot[:, 0:SLOTS] == slot_labels, jnp.broadcast_to(flag, (128, SLOTS)), 0.0)
    window_prob = jnp.where(in_first > 0.0, first_prob, second_prob).astype(BF16)
    placed = placement.astype(BF16)

    f = d * (1 - c) + y * c
    g = y * (1 - c) + d * c

    def at_fg(ff, gg):
        return (ff * (1 - c) + gg * c, gg * (1 - c) + ff * c)

    def device_fg(ff, gg):
        dd, yy = at_fg(ff % 4, gg % 4)
        return (dd, yy * 2 + c, s)

    def slot_fg(ff, gg):
        dd, yy = at_fg(ff % 4, gg % 4)
        return (dd * 8 + yy * 2 + c) * SLOTS

    own = row_range(slot_fg(f, g), SLOTS, SLOTS)
    rows[own, 0:FEATURES] = dot(placed, og[...], (0, 0)).astype(BF16)
    rows[own, FEATURES : FEATURES + TAIL] = dot(
        placed, jnp.broadcast_to(window_prob.astype(F32), (128, TAIL)).astype(BF16), (0, 0)
    ).astype(BF16)

    pl.semaphore_wait(barrier, 7)

    f_plus, f_minus = device_fg(f + 1, g), device_fg(f + 3, g)
    g_plus, g_minus = device_fg(f, g + 1), device_fg(f, g + 3)
    z_plus, z_minus = (d, e, (s + 1) % 16), (d, e, (s + 15) % 16)

    def pass_rows(ff, gg, target, part=None):
        first, count = slot_fg(ff, gg), SLOTS
        if part is not None:
            first, count = first + 16 * part, 16
        piece = rows.at[row_range(first, count, 16)]
        return start(piece, piece, target)

    def pass_weight(owner, part, target):
        piece = weight.at[row_range((owner % 16) * 192 + 96 * part, 96, 16)]
        return start(piece, piece, target)

    z_up = [[None, None] for _ in range(8)]
    z_down = [[None, None] for _ in range(8)]
    for part in range(2):
        z_up[0][part] = pass_weight(s, part, z_plus)
        z_down[0][part] = pass_weight(s, part, z_minus)
    to_f_plus = pass_rows(f, g, f_plus)
    to_f_minus = pass_rows(f, g, f_minus)
    g_up, g_down, g_up_half, g_down_half = [], [], [], []
    to_twin = []

    def spread_g(ff):
        g_up.append(pass_rows(ff, g, g_plus))
        g_down.append(pass_rows(ff, g, g_minus))
        to_twin.append(pass_rows(ff, g, twin))

    spread_g(f)

    low_in = dot(ctx[...], down[...], (1, 1)).astype(BF16)
    low_grad = (ADAPTER_SCALE * dot(og[...], up[...], (1, 1))).astype(BF16)
    adapt[0:RANK, :] = dot(low_in, og[...], (0, 0))
    adapt[RANK : 2 * RANK, :] = dot(low_grad, ctx[...], (0, 0))
    half = FEATURES // 2
    to_twin_a = start(
        adapt.at[:, pl.ds(pl.multiple_of((1 - c) * half, half), half)], a_twin, twin
    )

    def ring_step(h):
        for part in range(2):
            for chain, turn, target in ((z_up, -1, z_plus), (z_down, 1, z_minus)):
                if chain[h][part] is None:
                    continue
                chain[h][part].wait_recv()
                further = h + 1 < 7 or (h + 1 == 7 and part == (0 if chain is z_up else 1))
                if further:
                    chain[h + 1][part] = pass_weight(s + 16 + turn * (h + 1), part, target)

    from_f = (f, f + 3, f + 1, f + 2)

    def take_g(i):
        g_up[i].wait_recv()
        g_up_half.append(pass_rows(from_f[i], g + 3, g_plus, 0))
        g_down[i].wait_recv()
        g_down_half.append(pass_rows(from_f[i], g + 1, g_minus, 1))
        to_twin.append(pass_rows(from_f[i], g + 3, twin))
        to_twin.append(pass_rows(from_f[i], g + 1, twin))

    def take_g_half(i):
        g_up_half[i].wait_recv()
        g_down_half[i].wait_recv()
        to_twin.append(pass_rows(from_f[i], g + 2, twin))

    ring_step(0)
    to_f_plus.wait_recv()
    f_up_half = pass_rows(f + 3, g, f_plus, 0)
    spread_g(f + 3)
    to_f_minus.wait_recv()
    f_down_half = pass_rows(f + 1, g, f_minus, 1)
    spread_g(f + 1)
    ring_step(1)
    take_g(0)
    f_up_half.wait_recv()
    f_down_half.wait_recv()
    spread_g(f + 2)
    ring_step(2)
    take_g_half(0)
    ring_step(3)
    take_g(1)
    ring_step(4)
    take_g(2)
    take_g_half(1)
    ring_step(5)

    to_twin_a.wait_recv()
    a_twin[...] += adapt[:, pl.ds(pl.multiple_of(c * half, half), half)]
    a_y_out[...] = a_twin[...].astype(BF16)

    take_g(3)
    take_g_half(2)
    ring_step(6)
    take_g_half(3)
    a_y = []
    for j in range(1, 4):
        to = (y + j) % 4
        a_y.append(
            start(a_y_out.at[row_range(to * 32, 32, 32)], a_y_in.at[j - 1], (d, to * 2 + c, s))
        )
    for k in range(16):
        router_pad[k] = router[:, 192 * k : 192 * k + 192].astype(F32)
    up_router = dot(up[...], router[...], (1, 1))
    ring_step(7)
    for one in to_twin:
        one.wait_recv()

    exchange = []
    for j in (2, 1, 3, 0):
        to = (d + j) % 4
        product = dot(
            rows[row_range(to * 256, 256, 256), 0:FEATURES], weight[...], (1, 0)
        ).astype(BF16)
        if j == 0:
            prod_in[d] = product
        else:
            prod_out[to] = product
            exchange.append((j, start(prod_out.at[to], prod_in.at[d], (to, e, s))))

    for one in a_y:
        one.wait_recv()
    a_x_out[...] = a_twin[row_range(y * 32, 32, 32), :]
    for j in range(3):
        a_x_out[...] += a_y_in[j].astype(F32)
    a_x = []
    for j in range(1, 4):
        to = (d + j) % 4
        a_x.append(start(a_x_out.at[row_range(to * 8, 8, 8)], a_x_in.at[j - 1], (to, e, s)))

    own_probs = rows[row_range(d * 256, 256, 256), FEATURES : FEATURES + TAIL].astype(F32)

    def take_product(q, first):
        total = None
        for k in range(2):
            columns = pl.ds(pl.multiple_of(q * 256 + 128 * k, 128), 128)
            piece = prod_in[q, :, 128 * k : 128 * k + 128].astype(F32)
            hidden[:, columns] = (own_probs * piece).astype(BF16)
            term = stored[:, columns].astype(F32) * piece
            total = term if total is None else total + term
        if first:
            pg_out[...] = total
        else:
            pg_out[...] += total

    take_product(d, True)
    for j, one in exchange[1:] + exchange[:1]:
        one.wait_recv()
        take_product((d + 4 - j) % 4, False)
    hidden_copy = pltpu.make_async_copy(hidden, hidden_out, local.at[0])
    hidden_copy.start()

    pg = []
    for p in (4, 5, 3, 2, 6, 7, 1):
        to = (e + p) % 8
        pg.append(start(pg_out.at[row_range(to * 32, 32, 32)], pg_in.at[e], (d, to, s)))
    pg_in[e] = pg_out[row_range(e * 32, 32, 32), :]

    for one in a_x:
        one.wait_recv()
    part = a_x_out[row_range(d * 8, 8, 8), :] + a_x_in[0] + a_x_in[1] + a_x_in[2]
    for j in range(8):
        a_z_out[j, :, 0:192] = part[:, 192 * j : 192 * j + 192]
    a_z_out[:, :, 192:256] = jnp.zeros((8, 8, 64), F32)

    def over_z(out, landing):
        first_send, first_recv = used
        used[0] += 8
        used[1] += 16
        for j in range(8):
            k = c * 8 + j

            @pl.when(k != s)
            def _():
                describe(
                    out.at[j], landing.at[s], first_send + j, first_recv + s, (d, e, k)
                ).start()

        return first_send, first_recv

    def sum_over_z(out, landing, first):
        landing[s] = out[s % 8]
        for i in range(16):

            @pl.when(i != s)
            def _():
                describe(out.at[0], landing.at[i], first[0], first[1] + i, z_plus).wait_recv()

        total = landing[0]
        for i in range(1, 16):
            total = total + landing[i]
        return total

    def sent_over_z(out, first):
        for j in range(8):

            @pl.when(c * 8 + j != s)
            def _():
                describe(out.at[j], out.at[j], first[0] + j, first[1], z_plus).wait_send()

    first_a = over_z(a_z_out, a_z_in)

    for one in pg:
        one.wait_recv()
    returned = pg_in[0]
    for k in range(1, 8):
        returned = returned + pg_in[k]
    window_grad = jnp.sum(
        dot(placement, returned, (1, 0), lax.Precision.HIGHEST), axis=1, keepdims=True
    )
    spread = first_prob * second_prob * (window_grad * in_first - window_grad * in_second)
    sign = choose_first.astype(F32) - choose_second.astype(F32)
    logit_grad = (spread * sign).astype(BF16)

    by_feature = dot(logit_grad, ctx[...], (0, 0))
    by_rank = dot(logit_grad, low_in, (0, 0))
    for k in range(16):
        b_pad[k, :, 0:192] = by_feature[:, 192 * k : 192 * k + 192]
        b_pad[k, :, 192:256] = by_rank
    to_twin_b = start(b_pad.at[row_range((1 - c) * 8, 8, 8)], b_twin, twin)
    token[...] = dot(logit_grad, router[...], (1, 0)).astype(BF16)
    token_copy = pltpu.make_async_copy(token, token_out, local.at[1])
    token_copy.start()
    to_twin_b.wait_recv()
    b_z_out[...] = b_pad[row_range(c * 8, 8, 8)] + b_twin[...]
    first_b = over_z(b_z_out, b_z_in)

    first_y = list(used)
    first_x = [used[0] + 3, used[1] + 3]
    last = [used[0] + 6, used[1] + 6]

    @pl.when(keeps)
    def _():
        y_gather[y, 0:8, :] = sum_over_z(a_z_out, a_z_in, first_a)
        y_gather[y, 8:16, :] = sum_over_z(b_z_out, b_z_in, first_b)
        copies = []
        for j in range(1, 4):
            copies.append(
                describe(
                    y_gather.at[y],
                    y_gather.at[y],
                    first_y[0] + j - 1,
                    first_y[1] + j - 1,
                    (d, ((y + j) % 4) * 2 + c, s),
                )
            )
        for one in copies:
            one.start()
        for one in copies:
            one.wait_recv()
        for k in range(4):
            x_gather[d, 8 * k : 8 * k + 8, :] = y_gather[k, 0:8, :]
        x_gather[d, 32:40, :] = (
            y_gather[0, 8:16, :] + y_gather[1, 8:16, :] + y_gather[2, 8:16, :] + y_gather[3, 8:16, :]
        )
        for j in range(1, 4):
            copies.append(
                describe(
                    x_gather.at[d],
                    x_gather.at[d],
                    first_x[0] + j - 1,
                    first_x[1] + j - 1,
                    ((d + j) % 4, e, s),
                )
            )
        for one in copies[3:]:
            one.start()
        for one in copies[3:]:
            one.wait_recv()
        across = describe(x_gather, x_gather, last[0], last[1], twin)
        across.start()
        across.wait_send()
        for one in copies:
            one.wait_send()

    @pl.when(jnp.logical_not(keeps))
    def _():
        describe(x_gather, x_gather, last[0], last[1], twin).wait_recv()

    total = (
        x_gather[0, 32:40, :] + x_gather[1, 32:40, :] + x_gather[2, 32:40, :] + x_gather[3, 32:40, :]
    )
    exact = lax.Precision.HIGHEST
    more_up = dot(total[:, 192:256], router_pad[s], (0, 0), exact)
    more_down = dot(up_router, total[:, 0:192], (1, 0), exact)
    for k in range(4):
        for j in range(4):
            first = 32 * k + 8 * j
            block = x_gather[j, 8 * k : 8 * k + 8, 0:192]
            if k < 2:
                up_out[first : first + 8, :] = ADAPTER_SCALE * (block + more_up[first : first + 8])
            else:
                first = first - RANK
                down_out[first : first + 8, :] = block + ADAPTER_SCALE * more_down[first : first + 8]

    sent_over_z(a_z_out, first_a)
    sent_over_z(b_z_out, first_b)
    for one in made:
        one.wait_send()
    hidden_copy.wait()
    token_copy.wait()


def per_device(og, scores, idx, router, codes, scales, stored, ctx, down, up):
    vmem = pl.BlockSpec(memory_space=pltpu.VMEM)
    anywhere = pl.BlockSpec(memory_space=pl.ANY)
    shape = jax.ShapeDtypeStruct
    hidden_grad, token_grad, up_gradient, grad_down = pl.pallas_call(
        layer_kernel,
        out_shape=(
            shape((256, 1024), BF16),
            shape((128, FEATURES), BF16),
            shape((RANK, 192), F32),
            shape((RANK, 192), F32),
        ),
        in_specs=[vmem] * 10,
        out_specs=(anywhere, anywhere, vmem, vmem),
        scratch_shapes=[
            pltpu.VMEM((1024, FEATURES + TAIL), BF16),
            pltpu.VMEM((FEATURES, 256), BF16),
            pltpu.VMEM((4, 256, 256), BF16),
            pltpu.VMEM((4, 256, 256), BF16),
            pltpu.VMEM((256, 1024), BF16),
            pltpu.VMEM((128, FEATURES), BF16),
            pltpu.VMEM((256, 128), F32),
            pltpu.VMEM((8, 32, 128), F32),
            pltpu.VMEM((128, FEATURES), F32),
            pltpu.VMEM((128, FEATURES // 2), F32),
            pltpu.VMEM((128, FEATURES // 2), BF16),
            pltpu.VMEM((3, 32, FEATURES // 2), BF16),
            pltpu.VMEM((32, FEATURES // 2), F32),
            pltpu.VMEM((3, 8, FEATURES // 2), F32),
            pltpu.VMEM((8, 8, 256), F32),
            pltpu.VMEM((16, 8, 256), F32),
            pltpu.VMEM((16, 8, 256), F32),
            pltpu.VMEM((8, 8, 256), F32),
            pltpu.VMEM((8, 8, 256), F32),
            pltpu.VMEM((16, 8, 256), F32),
            pltpu.VMEM((4, 16, 256), F32),
            pltpu.VMEM((4, 40, 256), F32),
            pltpu.VMEM((16, 8, 192), F32),
            pltpu.SemaphoreType.DMA((SENDS,)),
            pltpu.SemaphoreType.DMA((RECVS,)),
            pltpu.SemaphoreType.DMA((2,)),
        ],
        compiler_params=pltpu.CompilerParams(
            collective_id=0, has_side_effects=True, vmem_limit_bytes=48 << 20
        ),
    )(og, scores, idx, router, codes, scales, stored[0, 0], ctx, down, up)
    return hidden_grad.reshape(stored.shape), token_grad, grad_down, up_gradient


def solution(mesh):
    tokens = P(("dp", "expert", "shard"), None)
    blocks = P("shard", "expert")
    hidden = P("dp", "shard", None, "expert")
    shares = P(None, "shard")
    return jax.shard_map(
        per_device,
        mesh=mesh,
        in_specs=(tokens, tokens, tokens, P(), blocks, blocks, hidden, tokens, P(), P()),
        out_specs=(hidden, tokens, shares, shares),
        check_vma=False,
    )
```

time: 640 us -> 90.6 us (0.14)
  waiting for transfers between devices: 576 us -> 0 us
  Pallas kernels: 0 us -> 78.7 us
  blocking collectives: 27.2 us -> 0 us
  between operations: 15.2 us -> 0.67 us
  matrix products: 13.4 us -> 0 us
  local copies, waits for them, and re-layouts: 3.95 us -> 10.8 us
    psum x1 -> x0, waiting for transfers between devices: 454 us -> none  [per_device(): lax.psum((partial_up_gradient, part_down), ('dp', 'expert', 'shard'))]
    all_gather x2 -> x0, waiting for transfers between devices: 122 us -> none  [the longest x1 86.7 us: per_device(): lax.all_gather(own_weight, 'shard', axis=0, tiled=True)]
    pallas_call x0 -> x1, Pallas kernels: none -> 78.7 us  [per_device(): pl.pallas_call(layer_kernel, out_shape=(shape((256, 1024), BF16), shape((...]
    unnamed x2 -> x0, blocking collectives: 27.2 us -> none
    dot_general x6 -> x0, matrix products: 13.4 us -> none  [the longest x1 5.16 us: per_device(): jnp.dot(all_rows, lax.all_gather(own_weight, 'shard', axis=0, tiled=True)...]
    unnamed x22 -> x24, local copies, waits for them, and re-layouts: 0.91 us -> 10.8 us
  transfers between devices with their start and end apart: 3 -> 0, of which waited for: 3 -> 0; matrix products, arithmetic and copies ran while one was open for 1% -> 0% of each run, Pallas kernels for 0% -> 0%
where the time goes in v2:
time: 90.6 us; the launch traced here: 90.2 us
  Pallas kernels  78.7 us (87%)
  local copies, waits for them, and re-layouts  10.8 us (12%)
    pallas_call x1, Pallas kernels, per_device(): pl.pallas_call(layer_kernel, out_shape=(shape((256, 1024), BF16), shape((...  78.7 us
    unnamed x24, local copies, waits for them, and re-layouts  10.8 us

profile of v2, /device:TPU:1, one launch (start us, length us, event | category | flops | bytes accessed | tf_op | source)
XLA Modules:
  0.0 90.2 jit_solution(15712950933322915816)
XLA Ops:
  0.6 0.0 copy-start.8
  0.6 0.8 copy.14.scores
  1.4 0.0 copy-done.8
  1.4 0.0 copy-start.6
  1.5 0.0 copy-start.7
  1.5 0.1 copy.15.idx
  1.6 0.7 copy-done.6
  2.2 0.0 copy-done.7
  2.2 0.0 copy-start
  2.2 1.1 %copy-done = bf16[128,3072]{1,0:T(8,128)(2,1)S(1)} copy-done((bf16[128,3072]{1,0:T(8,128)(2,1)S(1)}, bf16[128,3072]{1,0:T(8,128)(2,1)}, u32[]{:S(2)}) %copy-start) | copy-done | bytes 786456
  3.4 0.0 copy-start.1
  3.4 1.1 %copy-done.1 = bf16[128,3072]{1,0:T(8,128)(2,1)S(1)} copy-done((bf16[128,3072]{1,0:T(8,128)(2,1)S(1)}, bf16[128,3072]{1,0:T(8,128)(2,1)}, u32[]{:S(2)}) %copy-start.1) | copy-done | bytes 786456
  4.5 0.0 copy-start.2
  4.5 1.0 %copy-done.2 = bf16[1,1,256,1024]{3,2,1,0:T(8,128)(2,1)S(1)} copy-done((bf16[1,1,256,1024]{3,2,1,0:T(8,128)(2,1)S(1)}, bf16[1,1,256,1024]{3,2,1,0:T(8,128)(2,1)}, u32[]{:S(2)}) %copy-start.2) | copy-done | bytes 524312
  5.6 0.0 copy-start.3
  5.6 1.0 %copy-done.3 = bf16[192,1024]{1,0:T(8,128)(2,1)S(1)} copy-done((bf16[192,1024]{1,0:T(8,128)(2,1)S(1)}, bf16[192,1024]{1,0:T(8,128)(2,1)}, u32[]{:S(2)}) %copy-start.3) | copy-done | bytes 393240
  6.5 0.0 copy-start.4
  6.6 1.0 %copy-done.4 = bf16[64,3072]{1,0:T(8,128)(2,1)S(1)} copy-done((bf16[64,3072]{1,0:T(8,128)(2,1)S(1)}, bf16[64,3072]{1,0:T(8,128)(2,1)}, u32[]{:S(2)}) %copy-start.4) | copy-done | bytes 393240
  7.5 0.0 copy-start.5
  7.5 1.0 %copy-done.5 = bf16[64,3072]{1,0:T(8,128)(2,1)S(1)} copy-done((bf16[64,3072]{1,0:T(8,128)(2,1)S(1)}, bf16[64,3072]{1,0:T(8,128)(2,1)}, u32[]{:S(2)}) %copy-start.5) | copy-done | bytes 393240
  8.5 78.7 %shard_map.129 = (bf16[256,1024]{1,0:T(8,128)(2,1)S(1)}, bf16[128,3072]{1,0:T(8,128)(2,1)S(1)}, f32[64,192]{1,0:T(8,128)S(1)}, f32[64,192]{1,0:T(8,128)S(1)}) custom-call(bf16[128,3072]{1,0:T(8,128)(2,1)S(1)} %copy-done, f32[128,8]{1,0:T(8,128)S(1)} %copy.14.scores, s32[128,2]{1,0:T(8,128)S(1)} %copy.15.idx, bf16[8,3072]{1,0:T(8,128)(2,1)S(1)} %copy-done.6, ...), custom_call_target="tpu_custom_call" | custom-call | tf_op jit(solution)/shard_map/pallas_call | solution.py:461
  87.2 0.8 copy.20
  88.0 0.9 copy.21
  88.9 0.6 copy.22
  89.5 0.6 copy.23
Async XLA Ops:
  0.6 0.8 copy-start.8
  1.4 0.8 copy-start.6
  1.5 0.8 copy-start.7
  2.2 1.1 %copy-start = (bf16[128,3072]{1,0:T(8,128)(2,1)S(1)}, bf16[128,3072]{1,0:T(8,128)(2,1)}, u32[]{:S(2)}) copy-start(bf16[128,3072]{1,0:T(8,128)(2,1)} %og.1) | copy-start | bytes 2359300
  3.4 1.1 %copy-start.1 = (bf16[128,3072]{1,0:T(8,128)(2,1)S(1)}, bf16[128,3072]{1,0:T(8,128)(2,1)}, u32[]{:S(2)}) copy-start(bf16[128,3072]{1,0:T(8,128)(2,1)} %ctx.1) | copy-start | bytes 2359300
  4.5 1.0 %copy-start.2 = (bf16[1,1,256,1024]{3,2,1,0:T(8,128)(2,1)S(1)}, bf16[1,1,256,1024]{3,2,1,0:T(8,128)(2,1)}, u32[]{:S(2)}) copy-start(bf16[1,1,256,1024]{3,2,1,0:T(8,128)(2,1)} %param.16) | copy-start | bytes 1572868
  5.6 1.0 %copy-start.3 = (bf16[192,1024]{1,0:T(8,128)(2,1)S(1)}, bf16[192,1024]{1,0:T(8,128)(2,1)}, u32[]{:S(2)}) copy-start(bf16[192,1024]{1,0:T(8,128)(2,1)} %codes.1) | copy-start | bytes 1179652
  6.5 1.0 %copy-start.4 = (bf16[64,3072]{1,0:T(8,128)(2,1)S(1)}, bf16[64,3072]{1,0:T(8,128)(2,1)}, u32[]{:S(2)}) copy-start(bf16[64,3072]{1,0:T(8,128)(2,1)} %down.1) | copy-start | bytes 1179652
  7.5 1.0 %copy-start.5 = (bf16[64,3072]{1,0:T(8,128)(2,1)S(1)}, bf16[64,3072]{1,0:T(8,128)(2,1)}, u32[]{:S(2)}) copy-start(bf16[64,3072]{1,0:T(8,128)(2,1)} %up.1) | copy-start | bytes 1179652

commit v3 on v2

--- a/solution.py
+++ b/solution.py
@@ -19,20 +19,26 @@
 
 
 def layer_kernel(
-    og,
+    og_in,
     scores,
     idx,
     router,
+    codes_in,
+    scales,
+    stored_in,
+    ctx_in,
+    down_in,
+    up_in,
+    hidden_out,
+    token_out,
+    up_out,
+    down_out,
+    og,
     codes,
-    scales,
     stored,
     ctx,
     down,
     up,
-    hidden_out,
-    token_out,
-    up_out,
-    down_out,
     rows,
     weight,
     prod_out,
@@ -77,6 +83,20 @@
     ):
         pl.semaphore_signal(barrier, inc=1, device_id=target, device_id_type=MESH)
 
+    loads = []
+    for i, (src, dst) in enumerate(
+        (
+            (codes_in.at[:, pl.ds(pl.multiple_of(d * 256, 256), 256)], codes),
+            (og_in, og),
+            (ctx_in, ctx),
+            (down_in, down),
+            (up_in, up),
+            (stored_in, stored),
+        )
+    ):
+        loads.append(pltpu.make_async_copy(src, dst, local.at[2 + i]))
+        loads[-1].start()
+
     made = []
     used = [0, 0]
 
@@ -101,33 +121,35 @@
     def row_range(first, count, step):
         return pl.ds(pl.multiple_of(first, step), count)
 
-    quarter = pl.ds(pl.multiple_of(d * 256, 256), 256)
-    factors = scales[:, quarter].astype(F32)
-    for k in range(3):
-        block = codes[64 * k : 64 * k + 64, quarter].astype(F32) * factors[k : k + 1, :]
-        weight[row_range(s * 192 + 64 * k, 64, 64), :] = block.astype(BF16)
-
-    labels = lax.broadcasted_iota(jnp.int32, (128, 8), 1)
-    first_choice, second_choice = idx[:, 0:1], idx[:, 1:2]
+    labels = lax.broadcasted_iota(jnp.int32, (8, 128), 0)
+    first_choice, second_choice = idx[0:1, :], idx[1:2, :]
     choose_first, choose_second = labels == first_choice, labels == second_choice
     score = scores[...]
-    chosen_first = jnp.sum(jnp.where(choose_first, score, 0.0), axis=1, keepdims=True)
-    chosen_second = jnp.sum(jnp.where(choose_second, score, 0.0), axis=1, keepdims=True)
+    chosen_first = jnp.sum(jnp.where(choose_first, score, 0.0), axis=0, keepdims=True)
+    chosen_second = jnp.sum(jnp.where(choose_second, score, 0.0), axis=0, keepdims=True)
     first_prob = 1.0 / (1.0 + jnp.exp(chosen_second - chosen_first))
     second_prob = 1.0 - first_prob
     in_first = (first_choice == 0).astype(F32)
     in_second = (second_choice == 0).astype(F32)
     flag = in_first + in_second
-    before = lax.broadcasted_iota(jnp.int32, (128, 128), 0) > lax.broadcasted_iota(
+    before = lax.broadcasted_iota(jnp.int32, (128, 128), 0) < lax.broadcasted_iota(
         jnp.int32, (128, 128), 1
     )
     slot = dot(
-        before.astype(BF16), jnp.broadcast_to(flag, (128, 128)).astype(BF16), (1, 0)
-    )
-    slot_labels = lax.broadcasted_iota(jnp.int32, (128, SLOTS), 1).astype(F32)
-    placement = jnp.where(slot[:, 0:SLOTS] == slot_labels, jnp.broadcast_to(flag, (128, SLOTS)), 0.0)
-    window_prob = jnp.where(in_first > 0.0, first_prob, second_prob).astype(BF16)
-    placed = placement.astype(BF16)
+        jnp.broadcast_to(flag, (16, 128)).astype(BF16),
+        jnp.where(before, 1.0, 0.0).astype(BF16),
+        (1, 0),
+    )[0:1, :]
+    slot_labels = lax.broadcasted_iota(jnp.int32, (SLOTS, 128), 0).astype(F32)
+    placement = jnp.where(slot == slot_labels, flag, 0.0)
+    window_prob = jnp.where(in_first > 0.0, first_prob, second_prob).astype(BF16).astype(F32)
+
+    quarter = pl.ds(pl.multiple_of(d * 256, 256), 256)
+    factors = scales[:, quarter].astype(F32)
+    loads[0].wait()
+    for k in range(3):
+        block = codes[64 * k : 64 * k + 64, :].astype(F32) * factors[k : k + 1, :]
+        weight[row_range(s * 192 + 64 * k, 64, 64), :] = block.astype(BF16)
 
     f = d * (1 - c) + y * c
     g = y * (1 - c) + d * c
@@ -142,14 +164,6 @@
     def slot_fg(ff, gg):
         dd, yy = at_fg(ff % 4, gg % 4)
         return (dd * 8 + yy * 2 + c) * SLOTS
-
-    own = row_range(slot_fg(f, g), SLOTS, SLOTS)
-    rows[own, 0:FEATURES] = dot(placed, og[...], (0, 0)).astype(BF16)
-    rows[own, FEATURES : FEATURES + TAIL] = dot(
-        placed, jnp.broadcast_to(window_prob.astype(F32), (128, TAIL)).astype(BF16), (0, 0)
-    ).astype(BF16)
-
-    pl.semaphore_wait(barrier, 7)
 
     f_plus, f_minus = device_fg(f + 1, g), device_fg(f + 3, g)
     g_plus, g_minus = device_fg(f, g + 1), device_fg(f, g + 3)
@@ -166,11 +180,18 @@
         piece = weight.at[row_range((owner % 16) * 192 + 96 * part, 96, 16)]
         return start(piece, piece, target)
 
+    pl.semaphore_wait(barrier, 7)
     z_up = [[None, None] for _ in range(8)]
     z_down = [[None, None] for _ in range(8)]
     for part in range(2):
         z_up[0][part] = pass_weight(s, part, z_plus)
         z_down[0][part] = pass_weight(s, part, z_minus)
+    own = row_range(slot_fg(f, g), SLOTS, SLOTS)
+    loads[1].wait()
+    rows[own, 0:FEATURES] = dot(placement.astype(BF16), og[...], (1, 0)).astype(BF16)
+    rows[own, FEATURES : FEATURES + TAIL] = jnp.broadcast_to(
+        jnp.sum(placement * window_prob, axis=1, keepdims=True), (SLOTS, TAIL)
+    ).astype(BF16)
     to_f_plus = pass_rows(f, g, f_plus)
     to_f_minus = pass_rows(f, g, f_minus)
     g_up, g_down, g_up_half, g_down_half = [], [], [], []
@@ -183,6 +204,8 @@
 
     spread_g(f)
 
+    for one in loads[2:]:
+        one.wait()
     low_in = dot(ctx[...], down[...], (1, 1)).astype(BF16)
     low_grad = (ADAPTER_SCALE * dot(og[...], up[...], (1, 1))).astype(BF16)
     adapt[0:RANK, :] = dot(low_in, og[...], (0, 0))
@@ -358,20 +381,19 @@
     returned = pg_in[0]
     for k in range(1, 8):
         returned = returned + pg_in[k]
-    window_grad = jnp.sum(
-        dot(placement, returned, (1, 0), lax.Precision.HIGHEST), axis=1, keepdims=True
-    )
+    returned = jnp.sum(returned, axis=1, keepdims=True)
+    window_grad = jnp.sum(placement * returned, axis=0, keepdims=True)
     spread = first_prob * second_prob * (window_grad * in_first - window_grad * in_second)
     sign = choose_first.astype(F32) - choose_second.astype(F32)
     logit_grad = (spread * sign).astype(BF16)
 
-    by_feature = dot(logit_grad, ctx[...], (0, 0))
-    by_rank = dot(logit_grad, low_in, (0, 0))
+    by_feature = dot(logit_grad, ctx[...], (1, 0))
+    by_rank = dot(logit_grad, low_in, (1, 0))
     for k in range(16):
         b_pad[k, :, 0:192] = by_feature[:, 192 * k : 192 * k + 192]
         b_pad[k, :, 192:256] = by_rank
     to_twin_b = start(b_pad.at[row_range((1 - c) * 8, 8, 8)], b_twin, twin)
-    token[...] = dot(logit_grad, router[...], (1, 0)).astype(BF16)
+    token[...] = dot(logit_grad, router[...], (0, 0)).astype(BF16)
     token_copy = pltpu.make_async_copy(token, token_out, local.at[1])
     token_copy.start()
     to_twin_b.wait_recv()
@@ -454,21 +476,41 @@
     token_copy.wait()
 
 
+def finish_kernel(*refs):
+    sources, targets, held, done = refs[:4], refs[4:8], refs[8:12], refs[12]
+    loads = [pltpu.make_async_copy(sources[i], held[i], done.at[0, i]) for i in range(4)]
+    stores = [pltpu.make_async_copy(held[i], targets[i], done.at[1, i]) for i in range(4)]
+    for one in loads:
+        one.start()
+    for load, store in zip(loads, stores):
+        load.wait()
+        store.start()
+    for one in stores:
+        one.wait()
+
+
 def per_device(og, scores, idx, router, codes, scales, stored, ctx, down, up):
     vmem = pl.BlockSpec(memory_space=pltpu.VMEM)
     anywhere = pl.BlockSpec(memory_space=pl.ANY)
     shape = jax.ShapeDtypeStruct
-    hidden_grad, token_grad, up_gradient, grad_down = pl.pallas_call(
+    results = (
+        shape((256, 1024), BF16),
+        shape((128, FEATURES), BF16),
+        shape((RANK, 192), F32),
+        shape((RANK, 192), F32),
+    )
+    made = pl.pallas_call(
         layer_kernel,
-        out_shape=(
-            shape((256, 1024), BF16),
-            shape((128, FEATURES), BF16),
-            shape((RANK, 192), F32),
-            shape((RANK, 192), F32),
-        ),
-        in_specs=[vmem] * 10,
+        out_shape=results,
+        in_specs=[anywhere, vmem, vmem, vmem, anywhere, vmem] + [anywhere] * 4,
         out_specs=(anywhere, anywhere, vmem, vmem),
         scratch_shapes=[
+            pltpu.VMEM((128, FEATURES), BF16),
+            pltpu.VMEM((192, 256), BF16),
+            pltpu.VMEM((256, 1024), BF16),
+            pltpu.VMEM((128, FEATURES), BF16),
+            pltpu.VMEM((RANK, FEATURES), BF16),
+            pltpu.VMEM((RANK, FEATURES), BF16),
             pltpu.VMEM((1024, FEATURES + TAIL), BF16),
             pltpu.VMEM((FEATURES, 256), BF16),
             pltpu.VMEM((4, 256, 256), BF16),
@@ -494,12 +536,21 @@
             pltpu.VMEM((16, 8, 192), F32),
             pltpu.SemaphoreType.DMA((SENDS,)),
             pltpu.SemaphoreType.DMA((RECVS,)),
-            pltpu.SemaphoreType.DMA((2,)),
+            pltpu.SemaphoreType.DMA((8,)),
         ],
         compiler_params=pltpu.CompilerParams(
-            collective_id=0, has_side_effects=True, vmem_limit_bytes=48 << 20
+            collective_id=0, has_side_effects=True, vmem_limit_bytes=62 << 20
         ),
-    )(og, scores, idx, router, codes, scales, stored[0, 0], ctx, down, up)
+    )(og, scores.T, idx.T, router, codes, scales, stored[0, 0], ctx, down, up)
+    hidden_grad, token_grad, up_gradient, grad_down = pl.pallas_call(
+        finish_kernel,
+        out_shape=results,
+        in_specs=[anywhere] * 4,
+        out_specs=(anywhere,) * 4,
+        scratch_shapes=[pltpu.VMEM(one.shape, one.dtype) for one in results]
+        + [pltpu.SemaphoreType.DMA((2, 4))],
+        compiler_params=pltpu.CompilerParams(vmem_limit_bytes=62 << 20),
+    )(*made)
     return hidden_grad.reshape(stored.shape), token_grad, grad_down, up_gradient
 
 

time: 90.6 us -> 83.1 us (0.917)
  local copies, waits for them, and re-layouts: 10.8 us -> 0 us
  Pallas kernels: 78.7 us -> 82.3 us
    unnamed x24 -> x0, local copies, waits for them, and re-layouts: 10.8 us -> none
    pallas_call x1 -> x2, Pallas kernels: 78.7 us -> 82.3 us  [the longest x1 80 us: per_device(): pl.pallas_call(layer_kernel, out_shape=results, in_specs=[anywhere, vmem,...]
where the time goes in v3:
time: 83.1 us; the launch traced here: 82.9 us
  Pallas kernels  82.3 us (99%)
    pallas_call x1, Pallas kernels, per_device(): pl.pallas_call(layer_kernel, out_shape=results, in_specs=[anywhere, vmem,...  80 us
    pallas_call x1, Pallas kernels, per_device(): pl.pallas_call(finish_kernel, out_shape=results, in_specs=[anywhere] * 4,...  2.27 us

profile of v3, /device:TPU:1, one launch (start us, length us, event | category | flops | bytes accessed | tf_op | source)
XLA Modules:
  0.0 82.9 jit_solution(10190616431618292613)
XLA Ops:
  0.6 80.0 %shard_map.129 = (bf16[256,1024]{1,0:T(8,128)(2,1)}, bf16[128,3072]{1,0:T(8,128)(2,1)}, f32[64,192]{1,0:T(8,128)}, f32[64,192]{1,0:T(8,128)}) custom-call(bf16[128,3072]{1,0:T(8,128)(2,1)} %og_in.1, f32[8,128]{1,0:T(8,128)} %bitcast.5, s32[2,128]{1,0:T(2,128)} %bitcast.6, bf16[8,3072]{1,0:T(8,128)(2,1)} %router.1, bf16[192,1024]{1,0:T(8,128)(2,1)} %codes_in.1, ...), custom_call_target="tpu_custom_call" | custom-call | tf_op jit(solution)/shard_map/pallas_call | solution.py:502
  80.6 2.3 %shard_map.130 = (bf16[256,1024]{1,0:T(8,128)(2,1)}, bf16[128,3072]{1,0:T(8,128)(2,1)}, f32[64,192]{1,0:T(8,128)}, f32[64,192]{1,0:T(8,128)}) custom-call(bf16[256,1024]{1,0:T(8,128)(2,1)} %get-tuple-element.12.refs_0_, bf16[128,3072]{1,0:T(8,128)(2,1)} %get-tuple-element.13.refs_1_, f32[64,192]{1,0:T(8,128)} %get-tuple-element.14.refs_2_, ...), custom_call_target="tpu_custom_call" | custom-call | tf_op jit(solution)/shard_map/pallas_call | solution.py:545

commit v4 on v3

--- a/solution.py
+++ b/solution.py
@@ -9,7 +9,7 @@
 MESH = pl.DeviceIdType.MESH
 F32, BF16 = jnp.float32, jnp.bfloat16
 FEATURES, TAIL, SLOTS, RANK = 3072, 128, 32, 64
-SENDS, RECVS = 110, 130
+SENDS, RECVS = 120, 140
 
 
 def dot(a, b, over, precision=None):
@@ -59,9 +59,12 @@
     b_twin,
     b_z_out,
     b_z_in,
-    y_gather,
-    x_gather,
+    a_y_gather,
+    a_x_gather,
+    b_y_gather,
+    b_x_gather,
     router_pad,
+    twin_probs,
     send,
     recv,
     local,
@@ -78,8 +81,10 @@
         ((d + 3) % 4, e, s),
         (d, (e + 2) % 8, s),
         (d, (e + 6) % 8, s),
-        (d, e, (s + 1) % 16),
-        (d, e, (s + 15) % 16),
+        (d, y * 2, (s + 1) % 16),
+        (d, y * 2 + 1, (s + 1) % 16),
+        (d, y * 2, (s + 15) % 16),
+        (d, y * 2 + 1, (s + 15) % 16),
     ):
         pl.semaphore_signal(barrier, inc=1, device_id=target, device_id_type=MESH)
 
@@ -149,7 +154,7 @@
     loads[0].wait()
     for k in range(3):
         block = codes[64 * k : 64 * k + 64, :].astype(F32) * factors[k : k + 1, :]
-        weight[row_range(s * 192 + 64 * k, 64, 64), :] = block.astype(BF16)
+        weight[c, row_range(s * 192 + 64 * k, 64, 64), :] = block.astype(BF16)
 
     f = d * (1 - c) + y * c
     g = y * (1 - c) + d * c
@@ -161,46 +166,75 @@
         dd, yy = at_fg(ff % 4, gg % 4)
         return (dd, yy * 2 + c, s)
 
-    def slot_fg(ff, gg):
-        dd, yy = at_fg(ff % 4, gg % 4)
-        return (dd * 8 + yy * 2 + c) * SLOTS
-
     f_plus, f_minus = device_fg(f + 1, g), device_fg(f + 3, g)
     g_plus, g_minus = device_fg(f, g + 1), device_fg(f, g + 3)
-    z_plus, z_minus = (d, e, (s + 1) % 16), (d, e, (s + 15) % 16)
+    z_plus = (d, e, (s + 1) % 16)
 
     def pass_rows(ff, gg, target, part=None):
-        first, count = slot_fg(ff, gg), SLOTS
+        dd, yy = at_fg(ff % 4, gg % 4)
+        piece = rows.at[dd, yy]
         if part is not None:
-            first, count = first + 16 * part, 16
-        piece = rows.at[row_range(first, count, 16)]
+            piece = rows.at[dd, yy, pl.ds(16 * part, 16)]
         return start(piece, piece, target)
 
-    def pass_weight(owner, part, target):
-        piece = weight.at[row_range((owner % 16) * 192 + 96 * part, 96, 16)]
-        return start(piece, piece, target)
-
-    pl.semaphore_wait(barrier, 7)
-    z_up = [[None, None] for _ in range(8)]
-    z_down = [[None, None] for _ in range(8)]
+    def weight_piece(core, owner, part):
+        return weight.at[core, row_range((owner % 16) * 192 + 96 * part, 96, 16)]
+
+    turn = 1 - 2 * c
+    onward = (d, e, (s + 16 + turn) % 16)
+    pl.semaphore_wait(barrier, 9)
+    own_up, own_down = [], []
     for part in range(2):
-        z_up[0][part] = pass_weight(s, part, z_plus)
-        z_down[0][part] = pass_weight(s, part, z_minus)
-    own = row_range(slot_fg(f, g), SLOTS, SLOTS)
+        for core, step, made_first in ((0, 1, own_up), (1, 15, own_down)):
+            made_first.append(tuple(used))
+            used[0] += 1
+            used[1] += 2
+            piece = weight_piece(c, s, part)
+            describe(
+                piece,
+                piece,
+                made_first[-1][0],
+                made_first[-1][1] + c,
+                (d, y * 2 + core, (s + step) % 16),
+            ).start()
+    piece = weight.at[c, row_range(s * 192, 192, 64)]
+    weights_to_twin = [start(piece, piece, twin)]
+    passing = {}
+
+    def ring_step(h):
+        owner = s + 16 - turn * h
+        arrived = dict(passing)
+        passing.clear()
+        for part in range(2):
+            for core in range(2):
+                if h == 1:
+                    first = own_up[part][1] * (1 - c) + own_down[part][1] * c + core
+                    piece = weight_piece(core, owner, part)
+                    describe(piece, piece, 0, first, twin).wait_recv()
+                elif (core, part) in arrived:
+                    arrived[core, part].wait_recv()
+                if h < 7:
+                    piece = weight_piece(core, owner, part)
+                    passing[core, part] = start(piece, piece, onward)
+                elif h == 7 and core == 1:
+                    piece = weight_piece(c, owner, part)
+                    passing[core, part] = start(piece, piece, onward)
+        rows_of_owner = row_range((owner % 16) * 192, 192, 64)
+        piece = weight.at[:, rows_of_owner] if h < 8 else weight.at[c, rows_of_owner]
+        weights_to_twin.append(start(piece, piece, twin))
+
     loads[1].wait()
-    rows[own, 0:FEATURES] = dot(placement.astype(BF16), og[...], (1, 0)).astype(BF16)
-    rows[own, FEATURES : FEATURES + TAIL] = jnp.broadcast_to(
+    rows[d, y, :, 0:FEATURES] = dot(placement.astype(BF16), og[...], (1, 0)).astype(BF16)
+    rows[d, y, :, FEATURES : FEATURES + TAIL] = jnp.broadcast_to(
         jnp.sum(placement * window_prob, axis=1, keepdims=True), (SLOTS, TAIL)
     ).astype(BF16)
     to_f_plus = pass_rows(f, g, f_plus)
     to_f_minus = pass_rows(f, g, f_minus)
     g_up, g_down, g_up_half, g_down_half = [], [], [], []
-    to_twin = []
 
     def spread_g(ff):
         g_up.append(pass_rows(ff, g, g_plus))
         g_down.append(pass_rows(ff, g, g_minus))
-        to_twin.append(pass_rows(ff, g, twin))
 
     spread_g(f)
 
@@ -215,16 +249,6 @@
         adapt.at[:, pl.ds(pl.multiple_of((1 - c) * half, half), half)], a_twin, twin
     )
 
-    def ring_step(h):
-        for part in range(2):
-            for chain, turn, target in ((z_up, -1, z_plus), (z_down, 1, z_minus)):
-                if chain[h][part] is None:
-                    continue
-                chain[h][part].wait_recv()
-                further = h + 1 < 7 or (h + 1 == 7 and part == (0 if chain is z_up else 1))
-                if further:
-                    chain[h + 1][part] = pass_weight(s + 16 + turn * (h + 1), part, target)
-
     from_f = (f, f + 3, f + 1, f + 2)
 
     def take_g(i):
@@ -232,67 +256,44 @@
         g_up_half.append(pass_rows(from_f[i], g + 3, g_plus, 0))
         g_down[i].wait_recv()
         g_down_half.append(pass_rows(from_f[i], g + 1, g_minus, 1))
-        to_twin.append(pass_rows(from_f[i], g + 3, twin))
-        to_twin.append(pass_rows(from_f[i], g + 1, twin))
 
     def take_g_half(i):
         g_up_half[i].wait_recv()
         g_down_half[i].wait_recv()
-        to_twin.append(pass_rows(from_f[i], g + 2, twin))
-
-    ring_step(0)
+
+    ring_step(1)
     to_f_plus.wait_recv()
     f_up_half = pass_rows(f + 3, g, f_plus, 0)
     spread_g(f + 3)
     to_f_minus.wait_recv()
     f_down_half = pass_rows(f + 1, g, f_minus, 1)
     spread_g(f + 1)
-    ring_step(1)
+    ring_step(2)
     take_g(0)
+    ring_step(3)
     f_up_half.wait_recv()
     f_down_half.wait_recv()
     spread_g(f + 2)
-    ring_step(2)
+    ring_step(4)
     take_g_half(0)
-    ring_step(3)
-    take_g(1)
-    ring_step(4)
-    take_g(2)
-    take_g_half(1)
-    ring_step(5)
+    probs_to_twin = start(rows.at[d, :, :, pl.ds(FEATURES, TAIL)], twin_probs, twin)
 
     to_twin_a.wait_recv()
     a_twin[...] += adapt[:, pl.ds(pl.multiple_of(c * half, half), half)]
     a_y_out[...] = a_twin[...].astype(BF16)
-
-    take_g(3)
-    take_g_half(2)
-    ring_step(6)
-    take_g_half(3)
     a_y = []
     for j in range(1, 4):
         to = (y + j) % 4
         a_y.append(
             start(a_y_out.at[row_range(to * 32, 32, 32)], a_y_in.at[j - 1], (d, to * 2 + c, s))
         )
-    for k in range(16):
-        router_pad[k] = router[:, 192 * k : 192 * k + 192].astype(F32)
-    up_router = dot(up[...], router[...], (1, 1))
+
+    ring_step(5)
+    take_g(1)
+    ring_step(6)
+    take_g(2)
     ring_step(7)
-    for one in to_twin:
-        one.wait_recv()
-
-    exchange = []
-    for j in (2, 1, 3, 0):
-        to = (d + j) % 4
-        product = dot(
-            rows[row_range(to * 256, 256, 256), 0:FEATURES], weight[...], (1, 0)
-        ).astype(BF16)
-        if j == 0:
-            prod_in[d] = product
-        else:
-            prod_out[to] = product
-            exchange.append((j, start(prod_out.at[to], prod_in.at[d], (to, e, s))))
+    take_g_half(1)
 
     for one in a_y:
         one.wait_recv()
@@ -304,33 +305,30 @@
         to = (d + j) % 4
         a_x.append(start(a_x_out.at[row_range(to * 8, 8, 8)], a_x_in.at[j - 1], (to, e, s)))
 
-    own_probs = rows[row_range(d * 256, 256, 256), FEATURES : FEATURES + TAIL].astype(F32)
-
-    def take_product(q, first):
-        total = None
-        for k in range(2):
-            columns = pl.ds(pl.multiple_of(q * 256 + 128 * k, 128), 128)
-            piece = prod_in[q, :, 128 * k : 128 * k + 128].astype(F32)
-            hidden[:, columns] = (own_probs * piece).astype(BF16)
-            term = stored[:, columns].astype(F32) * piece
-            total = term if total is None else total + term
-        if first:
-            pg_out[...] = total
-        else:
-            pg_out[...] += total
-
-    take_product(d, True)
-    for j, one in exchange[1:] + exchange[:1]:
+    ring_step(8)
+    take_g(3)
+    take_g_half(2)
+    take_g_half(3)
+    for k in range(16):
+        router_pad[k] = router[:, 192 * k : 192 * k + 192].astype(F32)
+    up_router = dot(up[...], router[...], (1, 1))
+    for one in weights_to_twin:
         one.wait_recv()
-        take_product((d + 4 - j) % 4, False)
-    hidden_copy = pltpu.make_async_copy(hidden, hidden_out, local.at[0])
-    hidden_copy.start()
-
-    pg = []
-    for p in (4, 5, 3, 2, 6, 7, 1):
-        to = (e + p) % 8
-        pg.append(start(pg_out.at[row_range(to * 32, 32, 32)], pg_in.at[e], (d, to, s)))
-    pg_in[e] = pg_out[row_range(e * 32, 32, 32), :]
+
+    left = rows[:, :, :, 0:FEATURES].reshape(16 * SLOTS, FEATURES)
+    exchange = []
+    for k in range(2):
+        core = (c + 1 + k) % 2
+        product = dot(left, weight[core], (1, 0)).astype(BF16)
+        prod_out[k] = product.reshape(4, 128, 256)
+        for j in (2, 1, 3, 0):
+            to = (d + j) % 4
+            if j == 0 and k == 1:
+                prod_in[d, c] = prod_out[k, d]
+            else:
+                exchange.append(
+                    (j, k, start(prod_out.at[k, to], prod_in.at[d, c], (to, y * 2 + core, s)))
+                )
 
     for one in a_x:
         one.wait_recv()
@@ -375,6 +373,63 @@
                 describe(out.at[j], out.at[j], first[0] + j, first[1], z_plus).wait_send()
 
     first_a = over_z(a_z_out, a_z_in)
+
+    probs_to_twin.wait_recv()
+
+    def take_product(q, same, first):
+        core = c if same else 1 - c
+        for k in range(4):
+            place = pl.ds(pl.multiple_of(64 * k + 32 * core, 32), SLOTS)
+            prob = rows[d, k, :, FEATURES : FEATURES + TAIL] if same else twin_probs[k]
+            prob = prob.astype(F32)
+            total = None
+            for n in range(2):
+                columns = pl.ds(pl.multiple_of(q * 256 + 128 * n, 128), 128)
+                piece = prod_in[q, core, 32 * k : 32 * k + 32, 128 * n : 128 * n + 128].astype(F32)
+                hidden[place, columns] = (prob * piece).astype(BF16)
+                term = stored[place, columns].astype(F32) * piece
+                total = term if total is None else total + term
+            if first:
+                pg_out[place, :] = total
+            else:
+                pg_out[place, :] += total
+
+    take_product(d, True, True)
+    order = {(1, 0): 0, (3, 0): 1, (0, 0): 2, (2, 0): 3, (1, 1): 4, (3, 1): 5, (2, 1): 6}
+    for j, k, one in sorted(exchange, key=lambda item: order[item[:2]]):
+        one.wait_recv()
+        take_product((d + 4 - j) % 4, k == 1, (j, k) == (1, 0))
+    hidden_copy = pltpu.make_async_copy(hidden, hidden_out, local.at[0])
+    hidden_copy.start()
+
+    pg = []
+    for p in (4, 5, 3, 2, 6, 7, 1):
+        to = (e + p) % 8
+        pg.append(start(pg_out.at[row_range(to * 32, 32, 32)], pg_in.at[e], (d, to, s)))
+    pg_in[e] = pg_out[row_range(e * 32, 32, 32), :]
+
+    def reserve(sends, recvs):
+        first = tuple(used)
+        used[0] += sends
+        used[1] += recvs
+        return first
+
+    def along(buffer, first, axis):
+        mine, copies = (y if axis == "y" else d), []
+        for j in range(1, 4):
+            to = (d, ((y + j) % 4) * 2 + c, s) if axis == "y" else ((d + j) % 4, e, s)
+            piece = buffer.at[mine]
+            copies.append(describe(piece, piece, first[0] + j - 1, first[1] + j - 1, to))
+        return copies
+
+    sems_a_y, sems_a_x, sems_a_twin = reserve(3, 3), reserve(3, 3), reserve(1, 1)
+    sems_b_y, sems_b_x = reserve(3, 3), reserve(7, 4)
+
+    @pl.when(keeps)
+    def _():
+        a_y_gather[y] = sum_over_z(a_z_out, a_z_in, first_a)
+        for one in along(a_y_gather, sems_a_y, "y"):
+            one.start()
 
     for one in pg:
         one.wait_recv()
@@ -400,79 +455,83 @@
     b_z_out[...] = b_pad[row_range(c * 8, 8, 8)] + b_twin[...]
     first_b = over_z(b_z_out, b_z_in)
 
-    first_y = list(used)
-    first_x = [used[0] + 3, used[1] + 3]
-    last = [used[0] + 6, used[1] + 6]
+    a_across = describe(a_x_gather, a_x_gather, sems_a_twin[0], sems_a_twin[1], twin)
 
     @pl.when(keeps)
     def _():
-        y_gather[y, 0:8, :] = sum_over_z(a_z_out, a_z_in, first_a)
-        y_gather[y, 8:16, :] = sum_over_z(b_z_out, b_z_in, first_b)
-        copies = []
-        for j in range(1, 4):
-            copies.append(
-                describe(
-                    y_gather.at[y],
-                    y_gather.at[y],
-                    first_y[0] + j - 1,
-                    first_y[1] + j - 1,
-                    (d, ((y + j) % 4) * 2 + c, s),
-                )
-            )
+        for one in along(a_y_gather, sems_a_y, "y"):
+            one.wait()
+        for k in range(4):
+            a_x_gather[d, 8 * k : 8 * k + 8, :] = a_y_gather[k]
+        copies = along(a_x_gather, sems_a_x, "x")
         for one in copies:
             one.start()
-        for one in copies:
+
+    for made_first in own_up + own_down:
+        piece = weight_piece(c, s, 0)
+        describe(piece, piece, made_first[0], 0, twin).wait_send()
+    for one in made:
+        one.wait_send()
+    sent_over_z(a_z_out, first_a)
+    hidden_copy.wait()
+
+    @pl.when(keeps)
+    def _():
+        for one in along(a_x_gather, sems_a_x, "x"):
+            one.wait()
+        a_across.start()
+        b_y_gather[y] = sum_over_z(b_z_out, b_z_in, first_b)
+        by_y = along(b_y_gather, sems_b_y, "y")
+        for one in by_y:
+            one.start()
+        for one in by_y:
             one.wait_recv()
-        for k in range(4):
-            x_gather[d, 8 * k : 8 * k + 8, :] = y_gather[k, 0:8, :]
-        x_gather[d, 32:40, :] = (
-            y_gather[0, 8:16, :] + y_gather[1, 8:16, :] + y_gather[2, 8:16, :] + y_gather[3, 8:16, :]
-        )
-        for j in range(1, 4):
-            copies.append(
-                describe(
-                    x_gather.at[d],
-                    x_gather.at[d],
-                    first_x[0] + j - 1,
-                    first_x[1] + j - 1,
-                    ((d + j) % 4, e, s),
+        b_x_gather[d] = b_y_gather[0] + b_y_gather[1] + b_y_gather[2] + b_y_gather[3]
+        piece = b_x_gather.at[d]
+        by_x = []
+        for j in (2, 1, 3, 0):
+            for core in (c, 1 - c):
+                if j == 0 and core is c:
+                    continue
+                target = ((d + j) % 4, y * 2 + core, s)
+                by_x.append(
+                    describe(piece, piece, sems_b_x[0] + len(by_x), sems_b_x[1] + d, target)
                 )
-            )
-        for one in copies[3:]:
+        for one in by_x:
             one.start()
-        for one in copies[3:]:
-            one.wait_recv()
-        across = describe(x_gather, x_gather, last[0], last[1], twin)
-        across.start()
-        across.wait_send()
-        for one in copies:
+        for q in range(4):
+
+            @pl.when(q != d)
+            def _():
+                slot = b_x_gather.at[q]
+                describe(slot, slot, sems_b_x[0], sems_b_x[1] + q, twin).wait_recv()
+
+        for one in by_x + by_y:
             one.wait_send()
+        a_across.wait_send()
 
     @pl.when(jnp.logical_not(keeps))
     def _():
-        describe(x_gather, x_gather, last[0], last[1], twin).wait_recv()
-
-    total = (
-        x_gather[0, 32:40, :] + x_gather[1, 32:40, :] + x_gather[2, 32:40, :] + x_gather[3, 32:40, :]
-    )
+        a_across.wait_recv()
+        for q in range(4):
+            slot = b_x_gather.at[q]
+            describe(slot, slot, sems_b_x[0], sems_b_x[1] + q, twin).wait_recv()
+
+    total = b_x_gather[0] + b_x_gather[1] + b_x_gather[2] + b_x_gather[3]
     exact = lax.Precision.HIGHEST
     more_up = dot(total[:, 192:256], router_pad[s], (0, 0), exact)
     more_down = dot(up_router, total[:, 0:192], (1, 0), exact)
     for k in range(4):
         for j in range(4):
             first = 32 * k + 8 * j
-            block = x_gather[j, 8 * k : 8 * k + 8, 0:192]
+            block = a_x_gather[j, 8 * k : 8 * k + 8, 0:192]
             if k < 2:
                 up_out[first : first + 8, :] = ADAPTER_SCALE * (block + more_up[first : first + 8])
             else:
                 first = first - RANK
                 down_out[first : first + 8, :] = block + ADAPTER_SCALE * more_down[first : first + 8]
 
-    sent_over_z(a_z_out, first_a)
     sent_over_z(b_z_out, first_b)
-    for one in made:
-        one.wait_send()
-    hidden_copy.wait()
     token_copy.wait()
 
 
@@ -511,10 +570,10 @@
             pltpu.VMEM((128, FEATURES), BF16),
             pltpu.VMEM((RANK, FEATURES), BF16),
             pltpu.VMEM((RANK, FEATURES), BF16),
-            pltpu.VMEM((1024, FEATURES + TAIL), BF16),
-            pltpu.VMEM((FEATURES, 256), BF16),
-            pltpu.VMEM((4, 256, 256), BF16),
-            pltpu.VMEM((4, 256, 256), BF16),
+            pltpu.VMEM((4, 4, SLOTS, FEATURES + TAIL), BF16),
+            pltpu.VMEM((2, FEATURES, 256), BF16),
+            pltpu.VMEM((2, 4, 128, 256), BF16),
+            pltpu.VMEM((4, 2, 128, 256), BF16),
             pltpu.VMEM((256, 1024), BF16),
             pltpu.VMEM((128, FEATURES), BF16),
             pltpu.VMEM((256, 128), F32),
@@ -531,9 +590,12 @@
             pltpu.VMEM((8, 8, 256), F32),
             pltpu.VMEM((8, 8, 256), F32),
             pltpu.VMEM((16, 8, 256), F32),
-            pltpu.VMEM((4, 16, 256), F32),
-            pltpu.VMEM((4, 40, 256), F32),
+            pltpu.VMEM((4, 8, 256), F32),
+            pltpu.VMEM((4, 32, 256), F32),
+            pltpu.VMEM((4, 8, 256), F32),
+            pltpu.VMEM((4, 8, 256), F32),
             pltpu.VMEM((16, 8, 192), F32),
+            pltpu.VMEM((4, SLOTS, TAIL), BF16),
             pltpu.SemaphoreType.DMA((SENDS,)),
             pltpu.SemaphoreType.DMA((RECVS,)),
             pltpu.SemaphoreType.DMA((8,)),

time: 83.1 us -> 80.6 us (0.970)
  Pallas kernels: 82.3 us -> 79.8 us
    pallas_call x1, Pallas kernels: 80 us -> 77.5 us  [per_device(): pl.pallas_call(layer_kernel, out_shape=results, in_specs=[anywhere, vmem,...]
where the time goes in v4:
time: 80.6 us; the launch traced here: 80.4 us
  Pallas kernels  79.8 us (99%)
    pallas_call x1, Pallas kernels, per_device(): pl.pallas_call(layer_kernel, out_shape=results, in_specs=[anywhere, vmem,...  77.5 us
    pallas_call x1, Pallas kernels, per_device(): pl.pallas_call(finish_kernel, out_shape=results, in_specs=[anywhere] * 4,...  2.27 us

profile of v4, /device:TPU:1, one launch (start us, length us, event | category | flops | bytes accessed | tf_op | source)
XLA Modules:
  0.0 80.4 jit_solution(16730036207673971942)
XLA Ops:
  0.6 77.5 %shard_map.129 = (bf16[256,1024]{1,0:T(8,128)(2,1)}, bf16[128,3072]{1,0:T(8,128)(2,1)}, f32[64,192]{1,0:T(8,128)}, f32[64,192]{1,0:T(8,128)}) custom-call(bf16[128,3072]{1,0:T(8,128)(2,1)} %og_in.1, f32[8,128]{1,0:T(8,128)} %bitcast.5, s32[2,128]{1,0:T(2,128)} %bitcast.6, bf16[8,3072]{1,0:T(8,128)(2,1)} %router.1, bf16[192,1024]{1,0:T(8,128)(2,1)} %codes_in.1, ...), custom_call_target="tpu_custom_call" | custom-call | tf_op jit(solution)/shard_map/pallas_call | solution.py:561
  78.1 2.3 %shard_map.130 = (bf16[256,1024]{1,0:T(8,128)(2,1)}, bf16[128,3072]{1,0:T(8,128)(2,1)}, f32[64,192]{1,0:T(8,128)}, f32[64,192]{1,0:T(8,128)}) custom-call(bf16[256,1024]{1,0:T(8,128)(2,1)} %get-tuple-element.12.refs_0_, bf16[128,3072]{1,0:T(8,128)(2,1)} %get-tuple-element.13.refs_1_, f32[64,192]{1,0:T(8,128)} %get-tuple-element.14.refs_2_, ...), custom_call_target="tpu_custom_call" | custom-call | tf_op jit(solution)/shard_map/pallas_call | solution.py:607

commit v5 on v4

--- a/solution.py
+++ b/solution.py
@@ -20,11 +20,11 @@
 
 def layer_kernel(
     og_in,
-    scores,
-    idx,
-    router,
+    scores_in,
+    idx_in,
+    router_in,
     codes_in,
-    scales,
+    scales_in,
     stored_in,
     ctx_in,
     down_in,
@@ -34,7 +34,11 @@
     up_out,
     down_out,
     og,
+    scores,
+    idx,
+    router,
     codes,
+    scales,
     stored,
     ctx,
     down,
@@ -92,11 +96,15 @@
     for i, (src, dst) in enumerate(
         (
             (codes_in.at[:, pl.ds(pl.multiple_of(d * 256, 256), 256)], codes),
+            (scales_in, scales),
+            (idx_in, idx),
+            (scores_in, scores),
             (og_in, og),
             (ctx_in, ctx),
             (down_in, down),
             (up_in, up),
             (stored_in, stored),
+            (router_in, router),
         )
     ):
         loads.append(pltpu.make_async_copy(src, dst, local.at[2 + i]))
@@ -126,6 +134,83 @@
     def row_range(first, count, step):
         return pl.ds(pl.multiple_of(first, step), count)
 
+    quarter = pl.ds(pl.multiple_of(d * 256, 256), 256)
+    loads[0].wait()
+    loads[1].wait()
+    factors = scales[:, quarter].astype(F32)
+    for k in range(3):
+        block = codes[64 * k : 64 * k + 64, :].astype(F32) * factors[k : k + 1, :]
+        weight[c, row_range(s * 192 + 64 * k, 64, 64), :] = block.astype(BF16)
+
+    f = d * (1 - c) + y * c
+    g = y * (1 - c) + d * c
+
+    def at_fg(ff, gg):
+        return (ff * (1 - c) + gg * c, gg * (1 - c) + ff * c)
+
+    def device_fg(ff, gg):
+        dd, yy = at_fg(ff % 4, gg % 4)
+        return (dd, yy * 2 + c, s)
+
+    f_plus, f_minus = device_fg(f + 1, g), device_fg(f + 3, g)
+    g_plus, g_minus = device_fg(f, g + 1), device_fg(f, g + 3)
+    z_plus = (d, e, (s + 1) % 16)
+
+    def pass_rows(ff, gg, target, part=None):
+        dd, yy = at_fg(ff % 4, gg % 4)
+        piece = rows.at[dd, yy]
+        if part is not None:
+            piece = rows.at[dd, yy, pl.ds(16 * part, 16)]
+        return start(piece, piece, target)
+
+    def weight_piece(core, owner, part):
+        return weight.at[core, row_range((owner % 16) * 192 + 96 * part, 96, 16)]
+
+    turn = 1 - 2 * c
+    onward = (d, e, (s + 16 + turn) % 16)
+    pl.semaphore_wait(barrier, 9)
+    own_up, own_down = [], []
+    for part in range(2):
+        for core, step, made_first in ((0, 1, own_up), (1, 15, own_down)):
+            made_first.append(tuple(used))
+            used[0] += 1
+            used[1] += 2
+            piece = weight_piece(c, s, part)
+            describe(
+                piece,
+                piece,
+                made_first[-1][0],
+                made_first[-1][1] + c,
+                (d, y * 2 + core, (s + step) % 16),
+            ).start()
+    piece = weight.at[c, row_range(s * 192, 192, 64)]
+    weights_to_twin = [start(piece, piece, twin)]
+    passing = {}
+
+    def ring_step(h):
+        owner = s + 16 - turn * h
+        arrived = dict(passing)
+        passing.clear()
+        for part in range(2):
+            for core in range(2):
+                if h == 1:
+                    first = own_up[part][1] * (1 - c) + own_down[part][1] * c + core
+                    piece = weight_piece(core, owner, part)
+                    describe(piece, piece, 0, first, twin).wait_recv()
+                elif (core, part) in arrived:
+                    arrived[core, part].wait_recv()
+                if h < 7:
+                    piece = weight_piece(core, owner, part)
+                    passing[core, part] = start(piece, piece, onward)
+                elif h == 7 and core == 1:
+                    piece = weight_piece(c, owner, part)
+                    passing[core, part] = start(piece, piece, onward)
+        rows_of_owner = row_range((owner % 16) * 192, 192, 64)
+        piece = weight.at[:, rows_of_owner] if h < 8 else weight.at[c, rows_of_owner]
+        weights_to_twin.append(start(piece, piece, twin))
+
+    loads[2].wait()
+    loads[3].wait()
     labels = lax.broadcasted_iota(jnp.int32, (8, 128), 0)
     first_choice, second_choice = idx[0:1, :], idx[1:2, :]
     choose_first, choose_second = labels == first_choice, labels == second_choice
@@ -149,81 +234,7 @@
     placement = jnp.where(slot == slot_labels, flag, 0.0)
     window_prob = jnp.where(in_first > 0.0, first_prob, second_prob).astype(BF16).astype(F32)
 
-    quarter = pl.ds(pl.multiple_of(d * 256, 256), 256)
-    factors = scales[:, quarter].astype(F32)
-    loads[0].wait()
-    for k in range(3):
-        block = codes[64 * k : 64 * k + 64, :].astype(F32) * factors[k : k + 1, :]
-        weight[c, row_range(s * 192 + 64 * k, 64, 64), :] = block.astype(BF16)
-
-    f = d * (1 - c) + y * c
-    g = y * (1 - c) + d * c
-
-    def at_fg(ff, gg):
-        return (ff * (1 - c) + gg * c, gg * (1 - c) + ff * c)
-
-    def device_fg(ff, gg):
-        dd, yy = at_fg(ff % 4, gg % 4)
-        return (dd, yy * 2 + c, s)
-
-    f_plus, f_minus = device_fg(f + 1, g), device_fg(f + 3, g)
-    g_plus, g_minus = device_fg(f, g + 1), device_fg(f, g + 3)
-    z_plus = (d, e, (s + 1) % 16)
-
-    def pass_rows(ff, gg, target, part=None):
-        dd, yy = at_fg(ff % 4, gg % 4)
-        piece = rows.at[dd, yy]
-        if part is not None:
-            piece = rows.at[dd, yy, pl.ds(16 * part, 16)]
-        return start(piece, piece, target)
-
-    def weight_piece(core, owner, part):
-        return weight.at[core, row_range((owner % 16) * 192 + 96 * part, 96, 16)]
-
-    turn = 1 - 2 * c
-    onward = (d, e, (s + 16 + turn) % 16)
-    pl.semaphore_wait(barrier, 9)
-    own_up, own_down = [], []
-    for part in range(2):
-        for core, step, made_first in ((0, 1, own_up), (1, 15, own_down)):
-            made_first.append(tuple(used))
-            used[0] += 1
-            used[1] += 2
-            piece = weight_piece(c, s, part)
-            describe(
-                piece,
-                piece,
-                made_first[-1][0],
-                made_first[-1][1] + c,
-                (d, y * 2 + core, (s + step) % 16),
-            ).start()
-    piece = weight.at[c, row_range(s * 192, 192, 64)]
-    weights_to_twin = [start(piece, piece, twin)]
-    passing = {}
-
-    def ring_step(h):
-        owner = s + 16 - turn * h
-        arrived = dict(passing)
-        passing.clear()
-        for part in range(2):
-            for core in range(2):
-                if h == 1:
-                    first = own_up[part][1] * (1 - c) + own_down[part][1] * c + core
-                    piece = weight_piece(core, owner, part)
-                    describe(piece, piece, 0, first, twin).wait_recv()
-                elif (core, part) in arrived:
-                    arrived[core, part].wait_recv()
-                if h < 7:
-                    piece = weight_piece(core, owner, part)
-                    passing[core, part] = start(piece, piece, onward)
-                elif h == 7 and core == 1:
-                    piece = weight_piece(c, owner, part)
-                    passing[core, part] = start(piece, piece, onward)
-        rows_of_owner = row_range((owner % 16) * 192, 192, 64)
-        piece = weight.at[:, rows_of_owner] if h < 8 else weight.at[c, rows_of_owner]
-        weights_to_twin.append(start(piece, piece, twin))
-
-    loads[1].wait()
+    loads[4].wait()
     rows[d, y, :, 0:FEATURES] = dot(placement.astype(BF16), og[...], (1, 0)).astype(BF16)
     rows[d, y, :, FEATURES : FEATURES + TAIL] = jnp.broadcast_to(
         jnp.sum(placement * window_prob, axis=1, keepdims=True), (SLOTS, TAIL)
@@ -238,16 +249,10 @@
 
     spread_g(f)
 
-    for one in loads[2:]:
+    for one in loads[5:]:
         one.wait()
     low_in = dot(ctx[...], down[...], (1, 1)).astype(BF16)
     low_grad = (ADAPTER_SCALE * dot(og[...], up[...], (1, 1))).astype(BF16)
-    adapt[0:RANK, :] = dot(low_in, og[...], (0, 0))
-    adapt[RANK : 2 * RANK, :] = dot(low_grad, ctx[...], (0, 0))
-    half = FEATURES // 2
-    to_twin_a = start(
-        adapt.at[:, pl.ds(pl.multiple_of((1 - c) * half, half), half)], a_twin, twin
-    )
 
     from_f = (f, f + 3, f + 1, f + 2)
 
@@ -262,6 +267,7 @@
         g_down_half[i].wait_recv()
 
     ring_step(1)
+    adapt[0:RANK, :] = dot(low_in, og[...], (0, 0))
     to_f_plus.wait_recv()
     f_up_half = pass_rows(f + 3, g, f_plus, 0)
     spread_g(f + 3)
@@ -269,6 +275,11 @@
     f_down_half = pass_rows(f + 1, g, f_minus, 1)
     spread_g(f + 1)
     ring_step(2)
+    adapt[RANK : 2 * RANK, :] = dot(low_grad, ctx[...], (0, 0))
+    half = FEATURES // 2
+    to_twin_a = start(
+        adapt.at[:, pl.ds(pl.multiple_of((1 - c) * half, half), half)], a_twin, twin
+    )
     take_g(0)
     ring_step(3)
     f_up_half.wait_recv()
@@ -561,11 +572,15 @@
     made = pl.pallas_call(
         layer_kernel,
         out_shape=results,
-        in_specs=[anywhere, vmem, vmem, vmem, anywhere, vmem] + [anywhere] * 4,
+        in_specs=[anywhere] * 10,
         out_specs=(anywhere, anywhere, vmem, vmem),
         scratch_shapes=[
             pltpu.VMEM((128, FEATURES), BF16),
+            pltpu.VMEM((8, 128), F32),
+            pltpu.VMEM((2, 128), jnp.int32),
+            pltpu.VMEM((8, FEATURES), BF16),
             pltpu.VMEM((192, 256), BF16),
+            pltpu.VMEM((3, 1024), BF16),
             pltpu.VMEM((256, 1024), BF16),
             pltpu.VMEM((128, FEATURES), BF16),
             pltpu.VMEM((RANK, FEATURES), BF16),
@@ -598,7 +613,7 @@
             pltpu.VMEM((4, SLOTS, TAIL), BF16),
             pltpu.SemaphoreType.DMA((SENDS,)),
             pltpu.SemaphoreType.DMA((RECVS,)),
-            pltpu.SemaphoreType.DMA((8,)),
+            pltpu.SemaphoreType.DMA((12,)),
         ],
         compiler_params=pltpu.CompilerParams(
             collective_id=0, has_side_effects=True, vmem_limit_bytes=62 << 20

time: 80.6 us -> 79.9 us (level)
  no operation moved by 1% of the time
where the time goes in v5:
time: 79.9 us; the launch traced here: 79.7 us
  Pallas kernels  79.1 us (99%)
    pallas_call x1, Pallas kernels, per_device(): pl.pallas_call(layer_kernel, out_shape=results, in_specs=[anywhere] * 10,...  76.8 us
    pallas_call x1, Pallas kernels, per_device(): pl.pallas_call(finish_kernel, out_shape=results, in_specs=[anywhere] * 4,...  2.27 us

profile of v5, /device:TPU:1, one launch (start us, length us, event | category | flops | bytes accessed | tf_op | source)
XLA Modules:
  0.0 79.7 jit_solution(3588103520244258129)
XLA Ops:
  0.6 76.8 %shard_map.129 = (bf16[256,1024]{1,0:T(8,128)(2,1)}, bf16[128,3072]{1,0:T(8,128)(2,1)}, f32[64,192]{1,0:T(8,128)}, f32[64,192]{1,0:T(8,128)}) custom-call(bf16[128,3072]{1,0:T(8,128)(2,1)} %og_in.1, f32[8,128]{1,0:T(8,128)} %bitcast.5, s32[2,128]{1,0:T(2,128)} %bitcast.6, bf16[8,3072]{1,0:T(8,128)(2,1)} %router_in.1, bf16[192,1024]{1,0:T(8,128)(2,1)} %codes_in.1, ...), custom_call_target="tpu_custom_call" | custom-call | tf_op jit(solution)/shard_map/pallas_call | solution.py:572
  77.4 2.3 %shard_map.130 = (bf16[256,1024]{1,0:T(8,128)(2,1)}, bf16[128,3072]{1,0:T(8,128)(2,1)}, f32[64,192]{1,0:T(8,128)}, f32[64,192]{1,0:T(8,128)}) custom-call(bf16[256,1024]{1,0:T(8,128)(2,1)} %get-tuple-element.12.refs_0_, bf16[128,3072]{1,0:T(8,128)(2,1)} %get-tuple-element.13.refs_1_, f32[64,192]{1,0:T(8,128)} %get-tuple-element.14.refs_2_, ...), custom_call_target="tpu_custom_call" | custom-call | tf_op jit(solution)/shard_map/pallas_call | solution.py:622

commit v6 on v5

--- a/solution.py
+++ b/solution.py
@@ -320,26 +320,27 @@
     take_g(3)
     take_g_half(2)
     take_g_half(3)
-    for k in range(16):
-        router_pad[k] = router[:, 192 * k : 192 * k + 192].astype(F32)
-    up_router = dot(up[...], router[...], (1, 1))
     for one in weights_to_twin:
         one.wait_recv()
 
-    left = rows[:, :, :, 0:FEATURES].reshape(16 * SLOTS, FEATURES)
     exchange = []
-    for k in range(2):
-        core = (c + 1 + k) % 2
-        product = dot(left, weight[core], (1, 0)).astype(BF16)
-        prod_out[k] = product.reshape(4, 128, 256)
-        for j in (2, 1, 3, 0):
-            to = (d + j) % 4
-            if j == 0 and k == 1:
-                prod_in[d, c] = prod_out[k, d]
-            else:
-                exchange.append(
-                    (j, k, start(prod_out.at[k, to], prod_in.at[d, c], (to, y * 2 + core, s)))
-                )
+    for pair in ((2, 1), (3, 0)):
+        left = jnp.concatenate(
+            [rows[(d + j) % 4, :, :, 0:FEATURES].reshape(128, FEATURES) for j in pair], axis=0
+        )
+        for k in range(2):
+            core = (c + 1 + k) % 2
+            product = dot(left, weight[core], (1, 0)).astype(BF16)
+            for n, j in enumerate(pair):
+                to = (d + j) % 4
+                block = product[128 * n : 128 * n + 128]
+                if j == 0 and k == 1:
+                    prod_in[d, c] = block
+                else:
+                    prod_out[k, to] = block
+                    exchange.append(
+                        (j, k, start(prod_out.at[k, to], prod_in.at[d, c], (to, y * 2 + core, s)))
+                    )
 
     for one in a_x:
         one.wait_recv()
@@ -406,7 +407,7 @@
                 pg_out[place, :] += total
 
     take_product(d, True, True)
-    order = {(1, 0): 0, (3, 0): 1, (0, 0): 2, (2, 0): 3, (1, 1): 4, (3, 1): 5, (2, 1): 6}
+    order = {(1, 0): 0, (1, 1): 1, (2, 0): 2, (2, 1): 3, (0, 0): 4, (3, 0): 5, (3, 1): 6}
     for j, k, one in sorted(exchange, key=lambda item: order[item[:2]]):
         one.wait_recv()
         take_product((d + 4 - j) % 4, k == 1, (j, k) == (1, 0))
@@ -477,6 +478,10 @@
         copies = along(a_x_gather, sems_a_x, "x")
         for one in copies:
             one.start()
+
+    for k in range(16):
+        router_pad[k] = router[:, 192 * k : 192 * k + 192].astype(F32)
+    up_router = dot(up[...], router[...], (1, 1))
 
     for made_first in own_up + own_down:
         piece = weight_piece(c, s, 0)

time: 79.9 us -> 79.1 us (0.990)
  Pallas kernels: 79.1 us -> 78.3 us
where the time goes in v6:
time: 79.1 us; the launch traced here: 79 us
  Pallas kernels  78.3 us (99%)
    pallas_call x1, Pallas kernels, per_device(): pl.pallas_call(layer_kernel, out_shape=results, in_specs=[anywhere] * 10,...  76.1 us
    pallas_call x1, Pallas kernels, per_device(): pl.pallas_call(finish_kernel, out_shape=results, in_specs=[anywhere] * 4,...  2.27 us

profile of v6, /device:TPU:1, one launch (start us, length us, event | category | flops | bytes accessed | tf_op | source)
XLA Modules:
  0.0 79.0 jit_solution(9372074617239587854)
XLA Ops:
  0.6 76.1 %shard_map.129 = (bf16[256,1024]{1,0:T(8,128)(2,1)}, bf16[128,3072]{1,0:T(8,128)(2,1)}, f32[64,192]{1,0:T(8,128)}, f32[64,192]{1,0:T(8,128)}) custom-call(bf16[128,3072]{1,0:T(8,128)(2,1)} %og_in.1, f32[8,128]{1,0:T(8,128)} %bitcast.5, s32[2,128]{1,0:T(2,128)} %bitcast.6, bf16[8,3072]{1,0:T(8,128)(2,1)} %router_in.1, bf16[192,1024]{1,0:T(8,128)(2,1)} %codes_in.1, ...), custom_call_target="tpu_custom_call" | custom-call | tf_op jit(solution)/shard_map/pallas_call | solution.py:577
  76.7 2.3 %shard_map.130 = (bf16[256,1024]{1,0:T(8,128)(2,1)}, bf16[128,3072]{1,0:T(8,128)(2,1)}, f32[64,192]{1,0:T(8,128)}, f32[64,192]{1,0:T(8,128)}) custom-call(bf16[256,1024]{1,0:T(8,128)(2,1)} %get-tuple-element.12.refs_0_, bf16[128,3072]{1,0:T(8,128)(2,1)} %get-tuple-element.13.refs_1_, f32[64,192]{1,0:T(8,128)} %get-tuple-element.14.refs_2_, ...), custom_call_target="tpu_custom_call" | custom-call | tf_op jit(solution)/shard_map/pallas_call | solution.py:627
